TPU v7x, 32 devices: a whole 2x2x4 slice. The times are simulated.
32 devices in a mesh: dp: 16 (over z, x, core), exp: 2 (over y).
Axes of the slice: x: 2, y: 2, z: 4, core: 2. Of those that a mesh axis runs over, the one named last changes fastest.
Arguments:
- tokens: bfloat16 [4096, 1024], P(('dp', 'exp')), may hold values from -6 to 6
- cotangent: bfloat16 [4096, 1024], P(('dp', 'exp')), may hold values from -6 to 6
- doc_lengths: int32 [64, 3], P(('dp', 'exp')), may hold values from 1 to 48, 64 in all within a row
- routes: int32 [4096, 8], P(('dp', 'exp')), may hold values from 0 to 15, all different within a row; in each aligned block of 64 rows (0 to 63, 64 to 127, ...) at most 40 rows name the same one
- qkv_weight: float32 [1024, 2048], P(('dp', 'exp')), may hold values from -0.25 to 0.25
- qkv_mean: float32 [1024, 2048], P(('dp', 'exp')), may hold values from -128 to 128
- qkv_square: float32 [1024, 2048], P(('dp', 'exp')), may hold values from 1843.2 to 7372.8
- out_weight: float32 [1024, 1024], P(('dp', 'exp')), may hold values from -0.5 to 0.5
- out_mean: float32 [1024, 1024], P(('dp', 'exp')), may hold values from -40 to 40
- out_square: float32 [1024, 1024], P(('dp', 'exp')), may hold values from 163.84 to 655.36
- router_weight: float32 [1024, 16], P(('dp', 'exp')), may hold values from -0.09375 to 0.09375
- router_mean: float32 [1024, 16], P(('dp', 'exp')), may hold values from -512 to 512
- router_square: float32 [1024, 16], P(('dp', 'exp')), may hold values from 34816 to 139264
- norm_gains: float32 [1024, 2], P(('dp', 'exp')), may hold values from 0.5 to 1.5
- gains_mean: float32 [1024, 2], P(('dp', 'exp')), may hold values from -160 to 160
- gains_square: float32 [1024, 2], P(('dp', 'exp')), may hold values from 3276.8 to 13107.2
- in_weight: float32 [16, 1024, 1024], P('exp', 'dp'), may hold values from -0.1875 to 0.1875
- in_mean: float32 [16, 1024, 1024], P('exp', 'dp'), may hold values from -20 to 20
- in_square: float32 [16, 1024, 1024], P('exp', 'dp'), may hold values from 51.2 to 204.8
- down_weight: float32 [16, 1024, 512], P('exp', 'dp'), may hold values from -2 to 2
- down_mean: float32 [16, 1024, 512], P('exp', 'dp'), may hold values from -5 to 5
- down_square: float32 [16, 1024, 512], P('exp', 'dp'), may hold values from 0.57344 to 2.2528
Outputs:
- block_out: bfloat16 [4096, 1024], P(('dp', 'exp'))
- input_grad: bfloat16 [4096, 1024], P(('dp', 'exp'))
- new_qkv: float32 [1024, 2048], P(('dp', 'exp'))
- new_qkv_mean: float32 [1024, 2048], P(('dp', 'exp'))
- new_qkv_square: float32 [1024, 2048], P(('dp', 'exp'))
- new_out: float32 [1024, 1024], P(('dp', 'exp'))
- new_out_mean: float32 [1024, 1024], P(('dp', 'exp'))
- new_out_square: float32 [1024, 1024], P(('dp', 'exp'))
- new_router: float32 [1024, 16], P(('dp', 'exp'))
- new_router_mean: float32 [1024, 16], P(('dp', 'exp'))
- new_router_square: float32 [1024, 16], P(('dp', 'exp'))
- new_gains: float32 [1024, 2], P(('dp', 'exp'))
- new_gains_mean: float32 [1024, 2], P(('dp', 'exp'))
- new_gains_square: float32 [1024, 2], P(('dp', 'exp'))
- new_in: float32 [16, 1024, 1024], P('exp', 'dp')
- new_in_mean: float32 [16, 1024, 1024], P('exp', 'dp')
- new_in_square: float32 [16, 1024, 1024], P('exp', 'dp')
- new_down: float32 [16, 1024, 512], P('exp', 'dp')
- new_down_mean: float32 [16, 1024, 512], P('exp', 'dp')
- new_down_square: float32 [16, 1024, 512], P('exp', 'dp')
Inputs may be any that keep to these rules, and one draw needn't show every extreme that they name: `doc_lengths`: row b lists the lengths of the 3 documents of block b in order; they sum to 64, and the longest is exactly 48. `routes`: each row names 8 different experts. In each aligned block of 64 rows (one micro-batch of one device) no expert is named by more than 40 rows, a bound that some block reaches.
All inputs are finite; a program needn't handle non-finite values.
Results may differ from a plain program's by a relative error of at most 0.02.
Values may be sent and summed in bfloat16 or wider, within the bound.
No kernel may reach another device: no remote copies, remote signals or barrier semaphores. Data moves between devices by JAX's collectives and lax.ppermute only.
A program may use at most 192 MiB of HBM per device.

v0:
```python
import functools
import math

import jax
import jax.numpy as jnp
import numpy as np
from jax import lax
from jax.experimental import pallas as pl
from jax.experimental.pallas import tpu as pltpu
from jax.sharding import Mesh
from jax.sharding import PartitionSpec as P

QUERY_HEADS = 16
KEY_VALUE_HEADS = 8
HEAD_DIMENSION = 64
FF = 512
STEP = 10
EXPERTS = 16
LANES = 128
MESH_AXES = ("a", "r", "core", "exp")
VMEM_BYTES = 26 * 1024 * 1024


norm_eps = 1e-06
rope_base = 10000.0
mask_fill = -1e30
beta_one = 0.9
beta_two = 0.95
adam_eps = 1e-08
decay_rate = 0.1


def rms_scale(values):
    return lax.rsqrt(jnp.mean(values * values, axis=-1, keepdims=True) + norm_eps)


def doc_layout(doc_lens, sequence_length):
    row_index = jnp.arange(sequence_length, dtype=jnp.int32)
    doc_ends = jnp.cumsum(doc_lens, dtype=jnp.int32)
    passed = (row_index[:, None] >= doc_ends[None, :]).astype(jnp.int32)
    segment = jnp.sum(passed, axis=1, dtype=jnp.int32)
    starts = jnp.sum(passed * doc_lens[None, :], axis=1, dtype=jnp.int32)
    return ((row_index - starts).astype(jnp.float32), segment)


def rope_tables(positions, head_size):
    half_size = head_size // 2
    freq_index = jnp.arange(half_size, dtype=jnp.float32)
    inverse = jnp.exp(freq_index * (-2.0 * math.log(rope_base) / head_size))
    angles = positions[:, None] * inverse[None, :]
    return (jnp.cos(angles), jnp.sin(angles))


def adamw(weight, gradient, mean_old, square_old, step_rate, weight_decay):
    mean_new = beta_one * mean_old + (1.0 - beta_one) * gradient
    square_new = beta_two * square_old + (1.0 - beta_two) * gradient * gradient
    corrected = (
        mean_new
        / (1.0 - beta_one**STEP)
        / (jnp.sqrt(square_new / (1.0 - beta_two**STEP)) + adam_eps)
    )
    return (weight - step_rate * (corrected + weight_decay * weight), mean_new, square_new)

def dot_nn(left, right):
    return jnp.dot(left, right, preferred_element_type=jnp.float32)


def dot_nt(left, right):
    return lax.dot_general(left, right, (((1,), (1,)), ((), ())), preferred_element_type=jnp.float32)


def dot_tn(left, right):
    return lax.dot_general(left, right, (((0,), (0,)), ((), ())), preferred_element_type=jnp.float32)


def lane_iota(rows):
    return lax.broadcasted_iota(jnp.int32, (rows, LANES), 1)


def gain_rows(extra, experts):
    row = lax.broadcasted_iota(jnp.int32, (8, LANES), 0)
    pick = (lane_iota(8) == row + experts).astype(jnp.bfloat16)
    return dot_nt(jnp.where(row < 2, pick, jnp.zeros_like(pick)), extra)


def swap_halves(values):
    half = HEAD_DIMENSION // 2
    lower = lane_iota(values.shape[0]) % HEAD_DIMENSION < half
    return jnp.where(lower, pltpu.roll(values, LANES - half, 1), pltpu.roll(values, half, 1))


def column_sums(values, lane):
    high = values.astype(jnp.bfloat16)
    low = (values - high.astype(jnp.float32)).astype(jnp.bfloat16)
    place = (lane_iota(values.shape[0]) == lane).astype(jnp.bfloat16)
    return dot_tn(high, place) + dot_tn(low, place)


def head_block(index):
    return slice(index * HEAD_DIMENSION, (index + 1) * HEAD_DIMENSION)


def attention_forward(
    experts,
    copies,
    x_ref,
    w_ref,
    cos_ref,
    sin_ref,
    allow_ref,
    used_ref,
    order_ref,
    wide_ref,
    qkv_ref,
    sent_ref,
):
    f32, bf16 = jnp.float32, jnp.bfloat16
    rows, width = x_ref.shape
    query_width = QUERY_HEADS * HEAD_DIMENSION
    key_width = KEY_VALUE_HEADS * HEAD_DIMENSION
    qkv_width = query_width + 2 * key_width
    extra = w_ref[:, qkv_width + width :]
    gains = gain_rows(extra, experts)
    x = x_ref[...].astype(f32)
    normed = (x * rms_scale(x) * gains[0:1]).astype(bf16)
    cosine, sine = cos_ref[...], sin_ref[...]
    for start in range(0, qkv_width, 512):
        part = dot_nn(normed, w_ref[:, start : start + 512])
        for inner in range(0, 512, LANES):
            piece = part[:, inner : inner + LANES]
            if start + inner < query_width + key_width:
                piece = piece * cosine + swap_halves(piece) * sine
            qkv_ref[:, start + inner : start + inner + LANES] = piece.astype(bf16)
    allowed = allow_ref[...] > 0.0
    lane = lane_iota(rows)
    logs = jnp.zeros((rows, LANES), f32)
    fold = QUERY_HEADS // KEY_VALUE_HEADS
    for group in range(KEY_VALUE_HEADS):
        keys = qkv_ref[:, query_width + group * HEAD_DIMENSION : query_width + (group + 1) * HEAD_DIMENSION]
        values = qkv_ref[
            :,
            query_width + key_width + group * HEAD_DIMENSION : query_width
            + key_width
            + (group + 1) * HEAD_DIMENSION,
        ]
        outs = []
        for head in range(group * fold, (group + 1) * fold):
            scores = dot_nt(qkv_ref[:, head_block(head)], keys) * HEAD_DIMENSION ** (-0.5)
            scores = jnp.where(allowed, scores, mask_fill)
            peak = jnp.max(scores, axis=1, keepdims=True)
            log_total = peak + jnp.log(jnp.sum(jnp.exp(scores - peak), axis=1, keepdims=True))
            logs = jnp.where(lane == head, log_total, logs)
            outs.append(dot_nn(jnp.exp(scores - log_total).astype(bf16), values))
        start = qkv_width + group * LANES
        qkv_ref[:, start : start + LANES] = jnp.concatenate(outs, axis=1).astype(bf16)
    wide_ref[:, width : width + LANES] = logs
    hidden = x + dot_nt(qkv_ref[:, qkv_width:], w_ref[:, qkv_width : qkv_width + width])
    wide_ref[:, :width] = hidden
    second = (hidden * rms_scale(hidden) * gains[1:2]).astype(bf16)
    used = used_ref[...] > 0.0
    logits = jnp.where(used, dot_nn(second, extra), mask_fill)
    powers = jnp.where(used, jnp.exp(logits - jnp.max(logits, axis=1, keepdims=True)), 0.0)
    gates = powers / jnp.sum(powers, axis=1, keepdims=True)
    wide_ref[:, width + LANES :] = gates
    high = gates.astype(bf16).astype(f32)
    lanes = (high + pltpu.roll(gates - high, experts, 1)).astype(bf16)
    moved = dot_nn(second, order_ref[...]).astype(bf16)
    for copy in range(copies):
        sent_ref[copy, :, :width] = moved
        sent_ref[copy, :, width:] = lanes


def own_gate(lanes, number, experts):
    lane = lane_iota(lanes.shape[0])
    chosen = (lane == number) | (lane == number + experts)
    return jnp.sum(jnp.where(chosen, lanes.astype(jnp.float32), 0.0), axis=1, keepdims=True)


def experts_forward(
    experts, local_count, place_ref, rows_ref, w_ref, out_ref, inner_ref, sum_ref
):
    f32, bf16 = jnp.float32, jnp.bfloat16
    index, chunk = pl.program_id(0), pl.program_id(1)
    count, width = out_ref.shape
    gate = own_gate(rows_ref[:, width:], index * local_count + place_ref[0], experts)
    inner = dot_nn(rows_ref[:, :width], w_ref[0, :, : 2 * FF])
    inner_ref[0] = inner
    gate_part = inner[:, :FF]
    activation = (gate_part * jax.nn.sigmoid(gate_part) * inner[:, FF:]).astype(bf16)
    result = dot_nt(activation, w_ref[0, :, 2 * FF :]).astype(bf16).astype(f32)
    here = pl.ds(pl.multiple_of(chunk * count, count), count)

    @pl.when(index == 0)
    def _():
        sum_ref[here, :] = gate * result

    @pl.when(index > 0)
    def _():
        sum_ref[here, :] += gate * result

    out_ref[...] = sum_ref[here, :].astype(bf16)


def experts_backward(
    experts,
    local_count,
    place_ref,
    gates_ref,
    cot_ref,
    w_ref,
    inner_ref,
    back_ref,
    inner_grad_ref,
    act_ref,
    sum_ref,
    dots_sum_ref,
):
    f32, bf16 = jnp.float32, jnp.bfloat16
    index, chunk = pl.program_id(0), pl.program_id(1)
    count, width = cot_ref.shape
    number = index * local_count + place_ref[0]
    gate = own_gate(gates_ref[...], number, experts)
    gate_part = inner_ref[0, :, :FF]
    up_part = inner_ref[0, :, FF:]
    gate_sigmoid = jax.nn.sigmoid(gate_part)
    gate_silu = gate_part * gate_sigmoid
    activation = (gate_silu * up_part).astype(bf16).astype(f32)
    act_ref[0] = (gate * activation).astype(bf16)
    act_grad = dot_nn(cot_ref[...], w_ref[0, :, 2 * FF :])
    dots = jnp.sum(activation * act_grad, axis=1, keepdims=True)
    dots_high = dots.astype(bf16).astype(f32)
    lane = lane_iota(count)
    lanes = jnp.where(lane == number, dots_high, 0.0) + jnp.where(
        lane == number + experts, dots - dots_high, 0.0
    )
    act_grad = gate * act_grad
    inner_grad_ref[0, :, :FF] = (
        act_grad * up_part * gate_sigmoid * (1.0 + gate_part * (1.0 - gate_sigmoid))
    ).astype(bf16)
    inner_grad_ref[0, :, FF:] = (act_grad * gate_silu).astype(bf16)
    copy_grad = dot_nt(inner_grad_ref[0], w_ref[0, :, : 2 * FF])
    here = pl.ds(pl.multiple_of(chunk * count, count), count)

    @pl.when(index == 0)
    def _():
        sum_ref[here, :] = copy_grad
        dots_sum_ref[here, :] = lanes

    @pl.when(index > 0)
    def _():
        sum_ref[here, :] += copy_grad
        dots_sum_ref[here, :] += lanes

    back_ref[:, :width] = sum_ref[here, :].astype(bf16)
    back_ref[:, width:] = dots_sum_ref[here, :].astype(bf16)


def experts_weights(where_ref, rows_ref, inner_grad_ref, cot_ref, act_ref, *grad_refs):
    goal = pl.program_id(0)
    inner = dot_tn(rows_ref[...], inner_grad_ref[0]).astype(jnp.bfloat16)
    down = dot_tn(cot_ref[...], act_ref[0]).astype(jnp.bfloat16)
    for index, grad_ref in enumerate(grad_refs):

        @pl.when(goal == index)
        def _(grad_ref=grad_ref):
            grad_ref[:, : 2 * FF] = inner
            grad_ref[:, 2 * FF :] = down


def home_backward(
    experts,
    parts_ref,
    order_ref,
    cot_ref,
    wide_ref,
    w_ref,
    qkv_ref,
    x_ref,
    cos_ref,
    sin_ref,
    allow_ref,
    grad_ref,
    input_grad_ref,
    mid_ref,
    proj_ref,
):
    f32, bf16 = jnp.float32, jnp.bfloat16
    rows, width = x_ref.shape
    sources = parts_ref.shape[0]
    query_width = QUERY_HEADS * HEAD_DIMENSION
    key_width = KEY_VALUE_HEADS * HEAD_DIMENSION
    qkv_width = query_width + 2 * key_width
    fold = QUERY_HEADS // KEY_VALUE_HEADS
    score_scale = HEAD_DIMENSION ** (-0.5)
    extra = w_ref[:, qkv_width + width :]
    gains = gain_rows(extra, experts)
    dots = jnp.zeros((rows, LANES), f32)
    second_grad = jnp.zeros((rows, width), f32)
    for source in range(sources):
        dots = dots + parts_ref[source, :, width:].astype(f32)
        second_grad = second_grad + dot_nn(parts_ref[source, :, :width], order_ref[...])
    dots = dots + pltpu.roll(dots, LANES - experts, 1)
    gates = wide_ref[:, width + LANES :]
    logit_grad = (gates * (dots - jnp.sum(gates * dots, axis=1, keepdims=True))).astype(bf16)
    second_grad = second_grad + dot_nt(logit_grad, extra)
    hidden = wide_ref[:, :width]
    scale = rms_scale(hidden)
    second = (hidden * scale * gains[1:2]).astype(bf16)
    scaled = second_grad * gains[1:2]
    hidden_grad = (
        cot_ref[...].astype(f32)
        + scale * scaled
        - hidden * (scale * scale * scale) * jnp.mean(scaled * hidden, axis=1, keepdims=True)
    )
    branch_grad = hidden_grad.astype(bf16)
    for start in range(0, width, 512):
        grad_ref[:, qkv_width + start : qkv_width + start + 512] = dot_tn(
            branch_grad, qkv_ref[:, qkv_width + start : qkv_width + start + 512]
        ).astype(bf16)
    small_grad = dot_tn(second, logit_grad) + column_sums(
        second_grad * hidden * scale, experts + 1
    )
    mid_ref[...] = dot_nn(branch_grad, w_ref[:, qkv_width : qkv_width + width]).astype(bf16)
    cosine, sine = cos_ref[...], sin_ref[...]
    allowed = allow_ref[...] > 0.0
    lane = lane_iota(rows)
    logs = wide_ref[:, width : width + LANES]

    def turned_back(values):
        return (values * cosine - swap_halves(values) * sine).astype(bf16)

    key_grads, value_grads = [], []
    for group in range(KEY_VALUE_HEADS):
        keys = qkv_ref[:, query_width + group * HEAD_DIMENSION : query_width + (group + 1) * HEAD_DIMENSION]
        values = qkv_ref[
            :,
            query_width + key_width + group * HEAD_DIMENSION : query_width
            + key_width
            + (group + 1) * HEAD_DIMENSION,
        ]
        query_grads = []
        key_grad = jnp.zeros((rows, HEAD_DIMENSION), f32)
        value_grad = jnp.zeros((rows, HEAD_DIMENSION), f32)
        for head in range(group * fold, (group + 1) * fold):
            queries = qkv_ref[:, head_block(head)]
            mid = mid_ref[:, head_block(head)]
            log_total = jnp.sum(jnp.where(lane == head, logs, 0.0), axis=1, keepdims=True)
            scores = jnp.where(allowed, dot_nt(queries, keys) * score_scale, mask_fill)
            weights = jnp.exp(scores - log_total)
            weight_grad = dot_nt(mid, values)
            delta = jnp.sum(weights * weight_grad, axis=1, keepdims=True)
            score_grad = (weights * (weight_grad - delta)).astype(bf16)
            query_grads.append(dot_nn(score_grad, keys) * score_scale)
            key_grad = key_grad + dot_tn(score_grad, queries)
            value_grad = value_grad + dot_tn(weights.astype(bf16), mid)
        proj_ref[:, group * LANES : (group + 1) * LANES] = turned_back(
            jnp.concatenate(query_grads, axis=1)
        )
        key_grads.append(key_grad * score_scale)
        value_grads.append(value_grad)
        if group % 2 == 1:
            start = query_width + (group // 2) * LANES
            proj_ref[:, start : start + LANES] = turned_back(
                jnp.concatenate(key_grads[-2:], axis=1)
            )
            start = start + key_width
            proj_ref[:, start : start + LANES] = jnp.concatenate(value_grads[-2:], axis=1).astype(
                bf16
            )
    x = x_ref[...].astype(f32)
    scale = rms_scale(x)
    normed = (x * scale * gains[0:1]).astype(bf16)
    for start in range(0, qkv_width, 512):
        grad_ref[:, start : start + 512] = dot_tn(normed, proj_ref[:, start : start + 512]).astype(
            bf16
        )
    normed_grad = dot_nt(proj_ref[...], w_ref[:, :qkv_width])
    scaled = normed_grad * gains[0:1]
    small_grad = small_grad + column_sums(normed_grad * x * scale, experts)
    grad_ref[:, qkv_width + width :] = small_grad.astype(bf16)
    input_grad_ref[...] = (
        hidden_grad
        + scale * scaled
        - x * (scale * scale * scale) * jnp.mean(scaled * x, axis=1, keepdims=True)
    ).astype(bf16)


def dense_update(parts_ref, *refs):
    total = parts_ref[0].astype(jnp.float32)
    for source in range(1, parts_ref.shape[0]):
        total = total + parts_ref[source].astype(jnp.float32)
    start = total.shape[1] - LANES
    small = jnp.transpose(total[:, start:])
    experts = refs[6].shape[0]
    qkv_width = refs[0].shape[1]
    grads = (
        total[:, :qkv_width],
        total[:, qkv_width:start],
        small[:experts],
        small[experts : experts + 2],
    )
    rates = ((0.15, decay_rate), (0.3, decay_rate), (0.05, decay_rate), (0.8, 0.0))
    for index, (rate, decay) in enumerate(rates):
        weight_ref, mean_ref, square_ref = refs[3 * index : 3 * index + 3]
        values = adamw(weight_ref[...], grads[index], mean_ref[...], square_ref[...], rate, decay)
        for out_ref, value in zip(refs[3 * index + 12 : 3 * index + 15], values):
            out_ref[...] = value


def whole_call(kernel, outputs, operands, flops, scratch=(), earlier=()):
    operands_read = len(operands)

    def run(*refs):
        kernel(*refs[:operands_read], *refs[operands_read + len(earlier) :])

    moved = sum(math.prod(item.shape) * item.dtype.itemsize for item in list(outputs) + list(operands))
    moved = moved if flops > 1 else 1
    return pl.pallas_call(
        run,
        out_shape=outputs,
        in_specs=[pl.BlockSpec(memory_space=pltpu.VMEM)] * len(operands)
        + [pl.BlockSpec(memory_space=pl.ANY)] * len(earlier),
        out_specs=[pl.BlockSpec(memory_space=pltpu.VMEM)] * len(outputs),
        scratch_shapes=list(scratch),
        compiler_params=pltpu.CompilerParams(vmem_limit_bytes=VMEM_BYTES),
        cost_estimate=pl.CostEstimate(flops=flops, bytes_accessed=moved, transcendentals=0),
    )(*operands, *earlier)


def order_of(kind, sizes):
    axes = {"home": (0, 1, 2, 3, 4), "dense": (2, 1, 3, 0, 4), "expert": (1, 2, 0, 3, 4)}[kind]
    return np.arange(math.prod(sizes), dtype=np.int32).reshape(sizes).transpose(axes).reshape(-1)


def reorder_matrix(before, after):
    return (jnp.asarray(before)[:, None] == jnp.asarray(after)[None, :]).astype(jnp.bfloat16)


def exchange(values, axes):
    return lax.all_to_all(values, axes, split_axis=0, concat_axis=0, tiled=True)


def spread(values, axes):
    count = lax.axis_size(axes)
    copies = exchange(jnp.broadcast_to(values[None], (count,) + values.shape), axes)
    return copies.reshape((count * values.shape[0],) + values.shape[1:])


def collect(values, axes):
    count = lax.axis_size(axes)
    parts = exchange(values.reshape((count, values.shape[0] // count) + values.shape[1:]), axes)
    total = parts[0].astype(jnp.float32)
    for index in range(1, count):
        total = total + parts[index].astype(jnp.float32)
    return total


def partner(values, axes, step):
    names = (axes,) if isinstance(axes, str) else axes
    steps = {}
    for name in reversed(names):
        step, steps[name] = divmod(step, lax.axis_size(name))
    names = tuple(name for name in MESH_AXES if name in names)
    flat = 0
    for name in names:
        flat = flat * lax.axis_size(name) + steps[name]
    pairs = [(index, index ^ flat) for index in range(lax.axis_size(names))]
    return lax.ppermute(values, names, pairs)


def piece_of(values, index):
    return lax.dynamic_index_in_dim(values, index, 0, keepdims=False)


def in_order(own, received, me):
    result = jnp.zeros((len(received) + 1,) + own.shape, own.dtype)
    for step, part in enumerate([own] + received):
        result = lax.dynamic_update_index_in_dim(result, part, me ^ step, 0)
    return result


def spread_aside(values, axes):
    count = lax.axis_size(axes)
    received = [partner(values, axes, step) for step in range(1, count)]
    result = in_order(values, received, lax.axis_index(axes))
    return result.reshape((count * values.shape[0],) + values.shape[1:])


def pieces_for(values, axes):
    me = lax.axis_index(axes)
    return [piece_of(values, me ^ step) for step in range(values.shape[0])]


def exchange_aside(pieces, axes):
    received = [partner(piece, axes, step) for step, piece in enumerate(pieces) if step > 0]
    return in_order(pieces[0], received, lax.axis_index(axes))


def collect_aside(values, axes):
    count = lax.axis_size(axes)
    pieces = pieces_for(values.reshape((count, values.shape[0] // count) + values.shape[1:]), axes)
    total = pieces[0].astype(jnp.float32)
    for step in range(1, count):
        total = total + partner(pieces[step], axes, step).astype(jnp.float32)
    return total


def expert_specs(n_e, group_rows, width):
    count = min(256, group_rows)
    return dict(
        grid=(n_e, group_rows // count),
        scalar=pl.BlockSpec(memory_space=pltpu.SMEM),
        wide=pl.BlockSpec((count, width), lambda k, i: (i, 0)),
        wider=pl.BlockSpec((count, width + LANES), lambda k, i: (i, 0)),
        lanes=pl.BlockSpec((count, LANES), lambda k, i: (i, width // LANES)),
        weight=pl.BlockSpec((1, width, 3 * FF), lambda k, i: (k, 0, 0)),
        inner=pl.BlockSpec((1, count, 2 * FF), lambda k, i: (k, i, 0)),
        act=pl.BlockSpec((1, count, FF), lambda k, i: (k, i, 0)),
    )


def run_forward(place, arrived, expert_full, experts, local_count):
    n_e, width, _ = expert_full.shape
    group_rows = arrived.shape[0]
    specs = expert_specs(n_e, group_rows, width)
    return pl.pallas_call(
        functools.partial(experts_forward, experts, local_count),
        grid=specs["grid"],
        out_shape=[
            jax.ShapeDtypeStruct((group_rows, width), jnp.bfloat16),
            jax.ShapeDtypeStruct((n_e, group_rows, 2 * FF), jnp.float32),
        ],
        in_specs=[specs["scalar"], specs["wider"], specs["weight"]],
        out_specs=[specs["wide"], specs["inner"]],
        scratch_shapes=[pltpu.VMEM((group_rows, width), jnp.float32)],
        compiler_params=pltpu.CompilerParams(vmem_limit_bytes=VMEM_BYTES),
        cost_estimate=pl.CostEstimate(
            flops=2 * n_e * group_rows * width * 3 * FF,
            bytes_accessed=n_e * width * (3 * FF * 2 + group_rows * 8),
            transcendentals=n_e * group_rows * FF,
        ),
    )(place, arrived, expert_full)


def run_backward(place, arrived, cot_group, expert_full, inner, experts, local_count):
    bf16 = jnp.bfloat16
    n_e, width, _ = expert_full.shape
    group_rows = arrived.shape[0]
    specs = expert_specs(n_e, group_rows, width)
    return pl.pallas_call(
        functools.partial(experts_backward, experts, local_count),
        grid=specs["grid"],
        out_shape=[
            jax.ShapeDtypeStruct((group_rows, width + LANES), bf16),
            jax.ShapeDtypeStruct((n_e, group_rows, 2 * FF), bf16),
            jax.ShapeDtypeStruct((n_e, group_rows, FF), bf16),
        ],
        in_specs=[
            specs["scalar"],
            specs["lanes"],
            specs["wide"],
            specs["weight"],
            specs["inner"],
        ],
        out_specs=[specs["wider"], specs["inner"], specs["act"]],
        scratch_shapes=[
            pltpu.VMEM((group_rows, width), jnp.float32),
            pltpu.VMEM((group_rows, LANES), jnp.float32),
        ],
        compiler_params=pltpu.CompilerParams(vmem_limit_bytes=VMEM_BYTES),
        cost_estimate=pl.CostEstimate(
            flops=2 * n_e * group_rows * width * 3 * FF,
            bytes_accessed=n_e * width * (3 * FF * 2 + group_rows * 10),
            transcendentals=n_e * group_rows * FF,
        ),
    )(place, arrived, cot_group, expert_full, inner)


def run_weights(arrived, inner_grad, cot_group, act, slots, firsts, blocks, part):
    group_rows = arrived.shape[0]
    goals = len(slots)
    where = jnp.stack(slots + firsts).astype(jnp.int32)

    def block_of(index):
        return lambda g, j, at: (jnp.where(g == index, j, jnp.where(g < index, 0, blocks - 1)), 0)

    return pl.pallas_call(
        experts_weights,
        grid_spec=pltpu.PrefetchScalarGridSpec(
            num_scalar_prefetch=1,
            grid=(goals, blocks),
            in_specs=[
                pl.BlockSpec((group_rows, part), lambda g, j, at: (0, at[goals + g] + j)),
                pl.BlockSpec((1, group_rows, 2 * FF), lambda g, j, at: (at[g], 0, 0)),
                pl.BlockSpec((group_rows, part), lambda g, j, at: (0, at[goals + g] + j)),
                pl.BlockSpec((1, group_rows, FF), lambda g, j, at: (at[g], 0, 0)),
            ],
            out_specs=[pl.BlockSpec((part, 3 * FF), block_of(index)) for index in range(goals)],
        ),
        out_shape=[jax.ShapeDtypeStruct((blocks * part, 3 * FF), jnp.bfloat16)] * goals,
        compiler_params=pltpu.CompilerParams(vmem_limit_bytes=VMEM_BYTES),
        cost_estimate=pl.CostEstimate(
            flops=2 * goals * blocks * part * group_rows * 3 * FF,
            bytes_accessed=goals * (group_rows * 6 * FF + blocks * part * (group_rows * 4 + 6 * FF)),
            transcendentals=0,
        ),
    )(where, arrived, inner_grad, cot_group, act)


def in_pieces(n_e, n_r, width):
    return n_e * n_r <= 8 and width // n_r % min(256, width) == 0


def weight_grads(factors, n_e, n_r):
    width = factors[2].shape[1]
    part = min(256, width)
    if in_pieces(n_e, n_r, width):
        me = lax.axis_index(("exp", "r"))
        blocks = width // n_r // part
        goals = [me ^ step for step in range(n_e * n_r)]
        slots = [goal // n_r for goal in goals]
        firsts = [goal % n_r * blocks for goal in goals]
        return run_weights(*factors, slots, firsts, blocks, part)
    grads = []
    for slot in range(n_e):
        grads += run_weights(*factors, [jnp.int32(slot)], [jnp.int32(0)], width // part, part)
    return grads


def send_grads(grads, n_e, n_r, width):
    axes = ("exp", "r")
    if not in_pieces(n_e, n_r, width):
        grads = jnp.concatenate(grads, axis=0)
        return list(exchange(grads.reshape((n_e * n_r, -1) + grads.shape[1:]), axes))
    return [grads[0]] + [
        partner(grads[step], axes, step) for step in reversed(range(1, len(grads)))
    ]


def body(
    tokens,
    cotangent,
    doc_lengths,
    routes,
    qkv_weight,
    qkv_mean,
    qkv_square,
    out_weight,
    out_mean,
    out_square,
    router_weight,
    router_mean,
    router_square,
    norm_gains,
    gains_mean,
    gains_square,
    in_weight,
    in_mean,
    in_square,
    down_weight,
    down_mean,
    down_square,
):
    f32, bf16 = jnp.float32, jnp.bfloat16
    shape = jax.ShapeDtypeStruct
    n_a, n_r, n_c, n_e = (lax.axis_size(name) for name in ("a", "r", "core", "exp"))
    rows, width = tokens.shape
    experts = router_weight.shape[1]
    local_count = in_weight.shape[0]
    sizes = (n_a, n_r, n_c, n_e, width // (n_a * n_r * n_c * n_e))
    home, dense, expert = (order_of(kind, sizes) for kind in ("home", "dense", "expert"))
    query_width = QUERY_HEADS * HEAD_DIMENSION
    qkv_width = query_width + 2 * KEY_VALUE_HEADS * HEAD_DIMENSION

    local_rows = qkv_weight.shape[0]
    extra = jnp.zeros((local_rows, LANES - experts - 2), bf16)
    pack = jnp.concatenate(
        [
            qkv_weight.astype(bf16),
            out_weight.astype(bf16),
            router_weight.astype(bf16),
            norm_gains.astype(bf16),
            extra,
        ],
        axis=1,
    )
    pack = spread(pack, "a")

    to_dense = reorder_matrix(home, dense)
    x_dense = dot_nn(tokens, to_dense).astype(bf16)
    cot_dense = dot_nn(cotangent, to_dense).astype(bf16)
    positions, segment = doc_layout(doc_lengths.reshape(-1), rows)
    cosine, sine = rope_tables(positions, HEAD_DIMENSION)
    repeat = LANES // HEAD_DIMENSION
    cosine = jnp.concatenate([cosine, cosine] * repeat, axis=1)
    sine = jnp.concatenate([-sine, sine] * repeat, axis=1)
    row_index = jnp.arange(rows, dtype=jnp.int32)
    allowed = (segment[:, None] == segment[None, :]) & (row_index[None, :] <= row_index[:, None])
    allowed = allowed.astype(f32)
    used = jnp.any(
        routes[:, :, None] == jnp.arange(LANES, dtype=jnp.int32)[None, None, :], axis=1
    ).astype(f32)

    cot_expert = dot_nn(cotangent, reorder_matrix(home, expert)).astype(bf16)
    expert_pack = jnp.concatenate([in_weight.astype(bf16), down_weight.astype(bf16)], axis=2)
    to_expert = reorder_matrix(dense, expert)
    pieces = pieces_for(expert_pack, ("core", "a"))
    pack, x_dense, cot_dense, cosine, sine, allowed, used, to_expert, *pieces = (
        lax.optimization_barrier(
            (pack, x_dense, cot_dense, cosine, sine, allowed, used, to_expert, *pieces)
        )
    )
    pack = spread(pack, ("r", "exp"))
    expert_pack = exchange_aside(pieces, ("core", "a"))
    pack, expert_pack = lax.optimization_barrier((pack, expert_pack))
    cot_expert, expert_pack = lax.optimization_barrier((cot_expert, expert_pack))
    cot_group = spread_aside(spread_aside(cot_expert, "a"), "core")
    expert_full = lax.all_gather(expert_pack, ("exp", "r"), axis=0, tiled=True).reshape(
        n_e, width, 3 * FF
    )
    dense_full = spread(pack, "core")

    wide, qkv, sent = whole_call(
        functools.partial(attention_forward, experts, n_a),
        [
            shape((rows, width + 2 * LANES), f32),
            shape((rows, qkv_width + query_width), bf16),
            shape((n_a, rows, width + LANES), bf16),
        ],
        [x_dense, dense_full, cosine, sine, allowed, used, to_expert],
        flops=2 * rows * width * (qkv_width + 2 * width + 2 * rows),
    )

    arrived = exchange(sent, "a").reshape(n_a * rows, width + LANES)
    arrived = spread(arrived, "core")
    place = (lax.axis_index("core") * n_a + lax.axis_index("a")).astype(jnp.int32).reshape(1)
    out, inner = run_forward(place, arrived, expert_full, experts, local_count)
    back, inner_grad, activation = run_backward(
        place, arrived, cot_group, expert_full, inner, experts, local_count
    )
    out = collect_aside(out, "core").astype(bf16).reshape(n_a, rows, width)
    back = collect(back, "core").astype(bf16)

    factors = (arrived, inner_grad, cot_group, activation)
    expert_grads = list(weight_grads(factors, n_e, n_r))
    back = exchange(back.reshape(n_a, rows, width + LANES), "a")
    received = send_grads(expert_grads, n_e, n_r, width)
    back, out, expert_grads[0] = lax.optimization_barrier((back, out, expert_grads[0]))
    out = exchange(out, "a")

    from_expert = reorder_matrix(expert, dense)
    dense_grad, input_grad = whole_call(
        functools.partial(home_backward, experts),
        [shape((width, qkv_width + width + LANES), bf16), shape((rows, width), bf16)],
        [
            back,
            from_expert,
            cot_dense,
            wide,
            dense_full,
            qkv,
            x_dense,
            cosine,
            sine,
            allowed,
        ],
        earlier=expert_grads[:1],
        flops=1,
        scratch=[pltpu.VMEM((rows, query_width), bf16), pltpu.VMEM((rows, qkv_width), bf16)],
    )
    dense_grad, out = lax.optimization_barrier((dense_grad, out))
    dense_grad = collect(dense_grad, "core").astype(bf16)
    dense_grad, *received = lax.optimization_barrier((dense_grad, *received))
    expert_grad = received[0].astype(f32)
    for part in received[1:]:
        expert_grad = expert_grad + part.astype(f32)
    expert_grad = expert_grad.astype(bf16).reshape(
        n_c * n_a, width // (n_r * n_c * n_a), 3 * FF
    )
    expert_grad = exchange_aside(
        pieces_for(expert_grad, ("core", "a")), ("core", "a")
    ).astype(f32)
    d_in = expert_grad[:, :, : 2 * FF]
    d_down = expert_grad[:, :, 2 * FF :]
    dense_grad = collect(dense_grad, ("r", "exp")).astype(bf16)
    from_dense = reorder_matrix(dense, home)
    mixed = dot_nn(out[0], from_expert)
    for index in range(1, n_a):
        mixed = mixed + dot_nn(out[index], from_expert)
    block_out = dot_nn((wide[:, :width] + mixed).astype(bf16), from_dense).astype(bf16)
    input_grad = dot_nn(input_grad, from_dense).astype(bf16)
    dense_grad, block_out, input_grad = lax.optimization_barrier(
        (dense_grad, block_out, input_grad)
    )
    dense_grad = exchange(dense_grad.reshape((n_a, local_rows) + dense_grad.shape[1:]), "a")

    dense_state = [
        qkv_weight,
        qkv_mean,
        qkv_square,
        out_weight,
        out_mean,
        out_square,
        router_weight.T,
        router_mean.T,
        router_square.T,
        norm_gains.T,
        gains_mean.T,
        gains_square.T,
    ]
    (
        new_qkv,
        new_qkv_mean,
        new_qkv_square,
        new_out,
        new_out_mean,
        new_out_square,
        new_router,
        new_router_mean,
        new_router_square,
        new_gains,
        new_gains_mean,
        new_gains_square,
    ) = whole_call(
        dense_update,
        [shape(item.shape, f32) for item in dense_state],
        [dense_grad] + dense_state,
        flops=20 * local_rows * (qkv_width + width),
    )
    new_router, new_router_mean, new_router_square = (
        item.T for item in (new_router, new_router_mean, new_router_square)
    )
    new_gains, new_gains_mean, new_gains_square = (
        item.T for item in (new_gains, new_gains_mean, new_gains_square)
    )
    new_in, new_in_mean, new_in_square = adamw(in_weight, d_in, in_mean, in_square, 0.1, decay_rate)
    new_down, new_down_mean, new_down_square = adamw(
        down_weight, d_down, down_mean, down_square, 1.0, decay_rate
    )
    return (
        block_out,
        input_grad,
        new_qkv,
        new_qkv_mean,
        new_qkv_square,
        new_out,
        new_out_mean,
        new_out_square,
        new_router,
        new_router_mean,
        new_router_square,
        new_gains,
        new_gains_mean,
        new_gains_square,
        new_in,
        new_in_mean,
        new_in_square,
        new_down,
        new_down_mean,
        new_down_square,
    )


def attend_heads(experts, x_ref, w_ref, table_ref, allow_ref, qkv_ref, lse_ref, att_ref):
    f32, bf16 = jnp.float32, jnp.bfloat16
    rows = x_ref.shape[0]
    width = w_ref.shape[0]
    gains = gain_rows(w_ref[:, 2 * LANES :], experts)
    x = x_ref[:, :width].astype(f32)
    normed = (x * rms_scale(x) * gains[0:1]).astype(bf16)
    projected = dot_nn(normed, w_ref[:, : 2 * LANES])
    lane = lane_iota(rows)
    cosine, sine = table_ref[:, :LANES], table_ref[:, LANES:]
    queries, others = projected[:, :LANES], projected[:, LANES:]
    turned = others * cosine + swap_halves(others) * sine
    qkv_ref[:, :LANES] = (queries * cosine + swap_halves(queries) * sine).astype(bf16)
    qkv_ref[:, LANES:] = jnp.where(lane < HEAD_DIMENSION, turned, others).astype(bf16)
    keys = qkv_ref[:, LANES : LANES + HEAD_DIMENSION]
    values = qkv_ref[:, LANES + HEAD_DIMENSION :]
    allowed = allow_ref[0] > 0.0
    logs = jnp.zeros((rows, LANES), f32)
    outs = []
    for head in range(QUERY_HEADS // KEY_VALUE_HEADS):
        scores = dot_nt(qkv_ref[:, head_block(head)], keys) * HEAD_DIMENSION ** (-0.5)
        scores = jnp.where(allowed, scores, mask_fill)
        peak = jnp.max(scores, axis=1, keepdims=True)
        log_total = peak + jnp.log(jnp.sum(jnp.exp(scores - peak), axis=1, keepdims=True))
        logs = jnp.where(lane == head, log_total, logs)
        outs.append(dot_nn(jnp.exp(scores - log_total).astype(bf16), values))
    lse_ref[...] = logs
    att_ref[0] = jnp.concatenate(outs, axis=1).astype(bf16)


def home_forward(
    experts, copies, x_ref, att_ref, out_ref, extra_ref, used_ref, order_ref, wide_ref, sent_ref
):
    f32, bf16 = jnp.float32, jnp.bfloat16
    width = x_ref.shape[1]
    extra = extra_ref[...]
    hidden = x_ref[...].astype(f32)
    for place in range(att_ref.shape[0]):
        hidden = hidden + dot_nt(att_ref[place], out_ref[:, place * LANES : (place + 1) * LANES])
    wide_ref[:, :width] = hidden
    second = (hidden * rms_scale(hidden) * gain_rows(extra, experts)[1:2]).astype(bf16)
    used = used_ref[...] > 0.0
    logits = jnp.where(used, dot_nn(second, extra), mask_fill)
    powers = jnp.where(used, jnp.exp(logits - jnp.max(logits, axis=1, keepdims=True)), 0.0)
    gates = powers / jnp.sum(powers, axis=1, keepdims=True)
    wide_ref[:, width:] = gates
    high = gates.astype(bf16).astype(f32)
    lanes = (high + pltpu.roll(gates - high, experts, 1)).astype(bf16)
    moved = dot_nn(second, order_ref[...]).astype(bf16)
    for copy in range(copies):
        sent_ref[copy, :, :width] = moved
        sent_ref[copy, :, width:] = lanes


def home_back(
    experts,
    parts_ref,
    order_ref,
    cot_ref,
    wide_ref,
    extra_ref,
    out_ref,
    att_ref,
    split_ref,
    hidden_grad_ref,
    mid_ref,
    grad_ref,
):
    f32, bf16 = jnp.float32, jnp.bfloat16
    rows, width = cot_ref.shape
    extra = extra_ref[...]
    split = split_ref[...]
    dots = jnp.zeros((rows, LANES), f32)
    second_grad = jnp.zeros((rows, width), f32)
    for source in range(parts_ref.shape[0]):
        dots = dots + parts_ref[source, :, width:].astype(f32)
        second_grad = second_grad + dot_nn(parts_ref[source, :, :width], order_ref[...])
    dots = dots + pltpu.roll(dots, LANES - experts, 1)
    gates = wide_ref[:, width:]
    logit_grad = (gates * (dots - jnp.sum(gates * dots, axis=1, keepdims=True))).astype(bf16)
    second_grad = second_grad + dot_nt(logit_grad, extra)
    gain = gain_rows(extra, experts)[1:2]
    hidden = wide_ref[:, :width]
    scale = rms_scale(hidden)
    scaled = second_grad * gain
    hidden_grad = (
        cot_ref[...].astype(f32)
        + scale * scaled
        - hidden * (scale * scale * scale) * jnp.mean(scaled * hidden, axis=1, keepdims=True)
    )
    hidden_grad_ref[...] = hidden_grad
    branch_grad = hidden_grad.astype(bf16)
    branch_split = dot_nn(branch_grad, split).astype(bf16)
    for place in range(att_ref.shape[0]):
        columns = slice(place * LANES, (place + 1) * LANES)
        mid_ref[place] = dot_nn(branch_grad, out_ref[:, columns]).astype(bf16)
        grad_ref[:, columns] = dot_tn(branch_split, att_ref[place]).astype(bf16)
    second = dot_nn((hidden * scale * gain).astype(bf16), split).astype(bf16)
    sums = second_grad * hidden * scale
    high = sums.astype(bf16)
    low = (sums - high.astype(f32)).astype(bf16)
    place = (lane_iota(rows) == experts + 1).astype(bf16)
    grad_ref[:, width:] = (
        dot_tn(second, logit_grad)
        + dot_tn(dot_nn(high, split).astype(bf16), place)
        + dot_tn(dot_nn(low, split).astype(bf16), place)
    ).astype(bf16)


def heads_back(
    experts,
    x_ref,
    w_ref,
    table_ref,
    allow_ref,
    qkv_ref,
    lse_ref,
    mid_ref,
    grad_ref,
    normed_grad_ref,
    normed_ref,
    proj_ref,
    sums_ref,
):
    f32, bf16 = jnp.float32, jnp.bfloat16
    block = pl.program_id(0)
    rows = x_ref.shape[0]
    width = w_ref.shape[0]
    score_scale = HEAD_DIMENSION ** (-0.5)
    here = pl.ds(pl.multiple_of(block * rows, rows), rows)
    gains = gain_rows(w_ref[:, 2 * LANES :], experts)
    x = x_ref[:, :width].astype(f32)
    scale = rms_scale(x)
    normed_ref[here, :] = (x * scale * gains[0:1]).astype(bf16)
    keys = qkv_ref[:, LANES : LANES + HEAD_DIMENSION]
    values = qkv_ref[:, LANES + HEAD_DIMENSION :]
    allowed = allow_ref[0] > 0.0
    lane = lane_iota(rows)
    logs = lse_ref[...]
    query_grads = []
    key_grad = jnp.zeros((rows, HEAD_DIMENSION), f32)
    value_grad = jnp.zeros((rows, HEAD_DIMENSION), f32)
    for head in range(QUERY_HEADS // KEY_VALUE_HEADS):
        queries = qkv_ref[:, head_block(head)]
        mid = mid_ref[0, :, head_block(head)]
        log_total = jnp.sum(jnp.where(lane == head, logs, 0.0), axis=1, keepdims=True)
        scores = jnp.where(allowed, dot_nt(queries, keys) * score_scale, mask_fill)
        weights = jnp.exp(scores - log_total)
        weight_grad = dot_nt(mid, values)
        delta = jnp.sum(weights * weight_grad, axis=1, keepdims=True)
        score_grad = (weights * (weight_grad - delta)).astype(bf16)
        query_grads.append(dot_nn(score_grad, keys) * score_scale)
        key_grad = key_grad + dot_tn(score_grad, queries)
        value_grad = value_grad + dot_tn(weights.astype(bf16), mid)
    cosine, sine = table_ref[:, :LANES], table_ref[:, LANES:]
    queries = jnp.concatenate(query_grads, axis=1)
    others = jnp.concatenate([key_grad * score_scale, value_grad], axis=1)
    turned = others * cosine - swap_halves(others) * sine
    queries = (queries * cosine - swap_halves(queries) * sine).astype(bf16)
    others = jnp.where(lane < HEAD_DIMENSION, turned, others).astype(bf16)
    proj_ref[here, :] = jnp.concatenate([queries, others], axis=1)
    normed_grad = dot_nt(proj_ref[here, :], w_ref[:, : 2 * LANES])
    normed_grad_ref[0] = normed_grad.astype(bf16)
    sums = normed_grad * x * scale

    @pl.when(block == 0)
    def _():
        sums_ref[...] = sums

    @pl.when(block > 0)
    def _():
        sums_ref[...] += sums

    @pl.when(block == pl.num_programs(0) - 1)
    def _():
        grad_ref[:, : 2 * LANES] = dot_tn(normed_ref[...], proj_ref[...]).astype(bf16)
        grad_ref[:, 2 * LANES :] = column_sums(sums_ref[...], experts).astype(bf16)


def heads_update(places, qkv_parts_ref, out_parts_ref, *refs):
    f32 = jnp.float32
    sources = qkv_parts_ref.shape[0]
    totals = []
    for place in range(places):
        total = qkv_parts_ref[place].astype(f32)
        for source in range(place + places, sources, places):
            total = total + qkv_parts_ref[source].astype(f32)
        totals.append(total)
    out_total = out_parts_ref[0].astype(f32)
    for source in range(1, out_parts_ref.shape[0]):
        out_total = out_total + out_parts_ref[source].astype(f32)
    width = refs[3].shape[1]
    experts = refs[6].shape[0]
    small = out_total[:, width:]
    for total in totals:
        small = small + total[:, 2 * LANES :]
    small = jnp.transpose(small)
    middle = LANES + HEAD_DIMENSION
    qkv_grad = jnp.concatenate(
        [total[:, :LANES] for total in totals]
        + [total[:, LANES:middle] for total in totals]
        + [total[:, middle : 2 * LANES] for total in totals],
        axis=1,
    )
    grads = (qkv_grad, out_total[:, :width], small[:experts], small[experts : experts + 2])
    rates = ((0.15, decay_rate), (0.3, decay_rate), (0.05, decay_rate), (0.8, 0.0))
    for index, (rate, decay) in enumerate(rates):
        weight_ref, mean_ref, square_ref = refs[3 * index : 3 * index + 3]
        values = adamw(weight_ref[...], grads[index], mean_ref[...], square_ref[...], rate, decay)
        for out_ref, value in zip(refs[3 * index + 12 : 3 * index + 15], values):
            out_ref[...] = value


def block_call(kernel, blocks, inputs, outputs, operands, scratch, flops):
    def spec(shape, place):
        rank = len(shape)
        if place is None:
            return pl.BlockSpec(shape, lambda i: (0,) * rank)
        return pl.BlockSpec(shape, lambda i: (place(i),) + (0,) * (rank - 1))

    moved = sum(math.prod(item.shape) * item.dtype.itemsize for item in operands)
    return pl.pallas_call(
        kernel,
        grid=(blocks,),
        out_shape=[item for item, _, _ in outputs],
        in_specs=[spec(shape, place) for shape, place in inputs],
        out_specs=[spec(shape, place) for _, shape, place in outputs],
        scratch_shapes=scratch,
        compiler_params=pltpu.CompilerParams(vmem_limit_bytes=VMEM_BYTES),
        cost_estimate=pl.CostEstimate(flops=flops, bytes_accessed=moved, transcendentals=0),
    )(*operands)


def body_heads(
    tokens,
    cotangent,
    doc_lengths,
    routes,
    qkv_weight,
    qkv_mean,
    qkv_square,
    out_weight,
    out_mean,
    out_square,
    router_weight,
    router_mean,
    router_square,
    norm_gains,
    gains_mean,
    gains_square,
    in_weight,
    in_mean,
    in_square,
    down_weight,
    down_mean,
    down_square,
):
    f32, bf16 = jnp.float32, jnp.bfloat16
    shape = jax.ShapeDtypeStruct
    plane = ("r", "core", "exp")
    n_a, n_r, n_c, n_e = (lax.axis_size(name) for name in MESH_AXES)
    places = n_r * n_c * n_e
    rows, width = tokens.shape
    experts = router_weight.shape[1]
    local_count = in_weight.shape[0]
    local_rows = qkv_weight.shape[0]
    sizes = (n_a, n_r, n_c, n_e, local_rows)
    home, expert, split = (order_of(kind, sizes) for kind in ("home", "expert", "dense"))
    query_width = QUERY_HEADS * HEAD_DIMENSION
    key_width = KEY_VALUE_HEADS * HEAD_DIMENSION
    lines = places * local_rows

    positions, segment = doc_layout(doc_lengths.reshape(-1), rows)
    marks = jnp.stack([positions, segment.astype(f32)], axis=1).astype(bf16)
    marks = jnp.concatenate([marks, jnp.zeros((rows, LANES - 2), bf16)], axis=1)
    x_all = lax.all_gather(jnp.concatenate([tokens, marks], axis=1), plane, axis=0, tiled=True)

    def by_place(values, start, stop):
        return values[:, start:stop].reshape(local_rows, places, (stop - start) // places)

    qkv_low = qkv_weight.astype(bf16)
    extra = jnp.concatenate(
        [
            router_weight.astype(bf16),
            norm_gains.astype(bf16),
            jnp.zeros((local_rows, LANES - experts - 2), bf16),
        ],
        axis=1,
    )
    pack = jnp.concatenate(
        [
            by_place(qkv_low, 0, query_width),
            by_place(qkv_low, query_width, query_width + key_width),
            by_place(qkv_low, query_width + key_width, query_width + 2 * key_width),
            jnp.broadcast_to(extra[:, None], (local_rows, places, LANES)),
        ],
        axis=2,
    )
    pack = exchange(pack.transpose(1, 0, 2), plane).reshape(lines, 3 * LANES)
    pack = jnp.concatenate([pack, out_weight.astype(bf16).reshape(lines, LANES)], axis=1)
    pack = spread(pack, "a")
    out_full = pack[:, 3 * LANES :].reshape(n_a * local_rows, width)
    out_full = spread(spread(out_full, ("r", "exp")), "core")
    out_full = out_full.reshape(n_c, n_r, n_e, n_a, local_rows, width)
    out_full = out_full.transpose(3, 1, 0, 2, 4, 5).reshape(width, width)
    extra_full = pack[:, 2 * LANES : 3 * LANES]
    first_gain = extra_full[:, experts].astype(f32)

    expert_pack = jnp.concatenate([in_weight.astype(bf16), down_weight.astype(bf16)], axis=2)
    expert_pack = exchange_aside(pieces_for(expert_pack, ("core", "a")), ("core", "a"))
    cot_expert = dot_nn(cotangent, reorder_matrix(home, expert)).astype(bf16)
    cot_expert, expert_pack = lax.optimization_barrier((cot_expert, expert_pack))
    cot_group = spread_aside(spread_aside(cot_expert, "a"), "core")
    expert_full = lax.all_gather(expert_pack, ("exp", "r"), axis=0, tiled=True).reshape(
        n_e, width, 3 * FF
    )

    cosine, sine = rope_tables(x_all[:, width].astype(f32), HEAD_DIMENSION)
    repeat = LANES // HEAD_DIMENSION
    tables = jnp.concatenate([cosine, cosine] * repeat + [-sine, sine] * repeat, axis=1)
    segments = x_all[:, width + 1].astype(f32).reshape(places, rows)
    row_index = jnp.arange(rows, dtype=jnp.int32)
    allowed = (
        (segments[:, :, None] == segments[:, None, :])
        & (row_index[None, None, :] <= row_index[None, :, None])
    ).astype(f32)
    used = jnp.any(
        routes[:, :, None] == jnp.arange(LANES, dtype=jnp.int32)[None, None, :], axis=1
    ).astype(f32)

    def same(index):
        return index

    row_inputs = [
        ((rows, width + LANES), same),
        ((width, 3 * LANES), None),
        ((rows, 2 * LANES), same),
        ((1, rows, rows), same),
    ]
    qkv, logs, attended = block_call(
        functools.partial(attend_heads, experts),
        places,
        row_inputs,
        [
            (shape((places * rows, 2 * LANES), bf16), (rows, 2 * LANES), same),
            (shape((places * rows, LANES), f32), (rows, LANES), same),
            (shape((places, rows, LANES), bf16), (1, rows, LANES), same),
        ],
        [x_all, pack, tables, allowed],
        [],
        flops=2 * places * rows * width * 3 * LANES,
    )
    attended = exchange(attended, plane)
    wide, sent = whole_call(
        functools.partial(home_forward, experts, n_a),
        [shape((rows, width + LANES), f32), shape((n_a, rows, width + LANES), bf16)],
        [tokens, attended, out_full, extra_full, used, reorder_matrix(home, expert)],
        flops=4 * rows * width * width,
    )

    arrived = exchange(sent, "a").reshape(n_a * rows, width + LANES)
    arrived = spread(arrived, "core")
    place = (lax.axis_index("core") * n_a + lax.axis_index("a")).astype(jnp.int32).reshape(1)
    out, inner = run_forward(place, arrived, expert_full, experts, local_count)
    back, inner_grad, activation = run_backward(
        place, arrived, cot_group, expert_full, inner, experts, local_count
    )
    out = collect_aside(out, "core").astype(bf16).reshape(n_a, rows, width)
    back = collect(back, "core").astype(bf16)

    factors = (arrived, inner_grad, cot_group, activation)
    expert_grads = list(weight_grads(factors, n_e, n_r))
    back = exchange(back.reshape(n_a, rows, width + LANES), "a")
    received = send_grads(expert_grads, n_e, n_r, width)
    back, out, expert_grads[0] = lax.optimization_barrier((back, out, expert_grads[0]))
    out = exchange(out, "a")

    from_expert = reorder_matrix(expert, home)
    hidden_grad, mid, out_grad = whole_call(
        functools.partial(home_back, experts),
        [
            shape((rows, width), f32),
            shape((places, rows, LANES), bf16),
            shape((width, query_width + LANES), bf16),
        ],
        [
            back,
            from_expert,
            cotangent,
            wide,
            extra_full,
            out_full,
            attended,
            reorder_matrix(home, split),
        ],
        earlier=expert_grads[:1],
        flops=1,
    )
    mid, out = lax.optimization_barrier((mid, out))
    mid = exchange(mid, plane)

    def core_first(index):
        return (index // n_e % n_c * n_r + index // (n_c * n_e)) * n_e + index % n_e

    qkv_grad, normed_grad = block_call(
        functools.partial(heads_back, experts),
        places,
        row_inputs
        + [((rows, 2 * LANES), same), ((rows, LANES), same), ((1, rows, LANES), same)],
        [
            (shape((width, 3 * LANES), bf16), (width, 3 * LANES), None),
            (shape((places, rows, width), bf16), (1, rows, width), core_first),
        ],
        [x_all, pack, tables, allowed, qkv, logs, mid],
        [
            pltpu.VMEM((places * rows, width), bf16),
            pltpu.VMEM((places * rows, 2 * LANES), bf16),
            pltpu.VMEM((rows, width), f32),
        ],
        flops=2 * places * rows * width * 6 * LANES,
    )
    qkv_grad, out_grad = lax.optimization_barrier((qkv_grad, out_grad))
    qkv_grad = exchange(qkv_grad.reshape(n_a * places, local_rows, 3 * LANES), MESH_AXES)
    normed_grad = collect(normed_grad.reshape(places * rows, width), "core").astype(bf16)
    normed_grad = collect(normed_grad, ("r", "exp"))
    out_grad = collect(out_grad, "core").astype(bf16)
    qkv_grad, normed_grad, out_grad, *received = lax.optimization_barrier(
        (qkv_grad, normed_grad, out_grad, *received)
    )
    out_grad = collect(out_grad, ("r", "exp")).astype(bf16)
    out_grad = exchange(out_grad.reshape(n_a, local_rows, query_width + LANES), "a")

    residual = tokens.astype(f32)
    first_scale = rms_scale(residual)
    scaled = normed_grad * first_gain
    input_grad = (
        hidden_grad
        + first_scale * scaled
        - residual * first_scale**3 * jnp.mean(scaled * residual, axis=-1, keepdims=True)
    ).astype(bf16)
    mixed = dot_nn(out[0], from_expert)
    for index in range(1, n_a):
        mixed = mixed + dot_nn(out[index], from_expert)
    block_out = (wide[:, :width] + mixed).astype(bf16)

    expert_grad = received[0].astype(f32)
    for part in received[1:]:
        expert_grad = expert_grad + part.astype(f32)
    expert_grad = expert_grad.astype(bf16).reshape(
        n_c * n_a, width // (n_r * n_c * n_a), 3 * FF
    )
    expert_grad = exchange_aside(
        pieces_for(expert_grad, ("core", "a")), ("core", "a")
    ).astype(f32)
    d_in = expert_grad[:, :, : 2 * FF]
    d_down = expert_grad[:, :, 2 * FF :]

    dense_state = [
        qkv_weight,
        qkv_mean,
        qkv_square,
        out_weight,
        out_mean,
        out_square,
        router_weight.T,
        router_mean.T,
        router_square.T,
        norm_gains.T,
        gains_mean.T,
        gains_square.T,
    ]
    (
        new_qkv,
        new_qkv_mean,
        new_qkv_square,
        new_out,
        new_out_mean,
        new_out_square,
        new_router,
        new_router_mean,
        new_router_square,
        new_gains,
        new_gains_mean,
        new_gains_square,
    ) = whole_call(
        functools.partial(heads_update, places),
        [shape(item.shape, f32) for item in dense_state],
        [qkv_grad, out_grad] + dense_state,
        flops=60 * local_rows * width,
    )
    new_router, new_router_mean, new_router_square = (
        item.T for item in (new_router, new_router_mean, new_router_square)
    )
    new_gains, new_gains_mean, new_gains_square = (
        item.T for item in (new_gains, new_gains_mean, new_gains_square)
    )
    new_in, new_in_mean, new_in_square = adamw(in_weight, d_in, in_mean, in_square, 0.1, decay_rate)
    new_down, new_down_mean, new_down_square = adamw(
        down_weight, d_down, down_mean, down_square, 1.0, decay_rate
    )
    return (
        block_out,
        input_grad,
        new_qkv,
        new_qkv_mean,
        new_qkv_square,
        new_out,
        new_out_mean,
        new_out_square,
        new_router,
        new_router_mean,
        new_router_square,
        new_gains,
        new_gains_mean,
        new_gains_square,
        new_in,
        new_in_mean,
        new_in_square,
        new_down,
        new_down_mean,
        new_down_square,
    )


def solution(mesh):
    n_dp, n_exp = mesh.shape["dp"], mesh.shape["exp"]
    n_a = EXPERTS // n_exp // 2
    mesh = Mesh(
        mesh.devices.reshape(n_a, n_dp // (2 * n_a), 2, n_exp), MESH_AXES
    )
    placed = (
        P(("a", "r", "core", "exp"), None),
        P(("a", "r", "core", "exp"), None),
        P(("a", "r", "core", "exp"), None),
        P(("a", "r", "core", "exp"), None),
        P(("a", "r", "core", "exp"), None),
        P(("a", "r", "core", "exp"), None),
        P(("a", "r", "core", "exp"), None),
        P(("a", "r", "core", "exp"), None),
        P(("a", "r", "core", "exp"), None),
        P(("a", "r", "core", "exp"), None),
        P(("a", "r", "core", "exp"), None),
        P(("a", "r", "core", "exp"), None),
        P(("a", "r", "core", "exp"), None),
        P(("a", "r", "core", "exp"), None),
        P(("a", "r", "core", "exp"), None),
        P(("a", "r", "core", "exp"), None),
        P("exp", ("a", "r", "core"), None),
        P("exp", ("a", "r", "core"), None),
        P("exp", ("a", "r", "core"), None),
        P("exp", ("a", "r", "core"), None),
        P("exp", ("a", "r", "core"), None),
        P("exp", ("a", "r", "core"), None),
    )
    shared = mesh.size // n_a == KEY_VALUE_HEADS
    return jax.shard_map(
        body_heads if shared else body,
        mesh=mesh,
        in_specs=placed,
        out_specs=(
            P(("a", "r", "core", "exp"), None),
            P(("a", "r", "core", "exp"), None),
            P(("a", "r", "core", "exp"), None),
            P(("a", "r", "core", "exp"), None),
            P(("a", "r", "core", "exp"), None),
            P(("a", "r", "core", "exp"), None),
            P(("a", "r", "core", "exp"), None),
            P(("a", "r", "core", "exp"), None),
            P(("a", "r", "core", "exp"), None),
            P(("a", "r", "core", "exp"), None),
            P(("a", "r", "core", "exp"), None),
            P(("a", "r", "core", "exp"), None),
            P(("a", "r", "core", "exp"), None),
            P(("a", "r", "core", "exp"), None),
            P("exp", ("a", "r", "core"), None),
            P("exp", ("a", "r", "core"), None),
            P("exp", ("a", "r", "core"), None),
            P("exp", ("a", "r", "core"), None),
            P("exp", ("a", "r", "core"), None),
            P("exp", ("a", "r", "core"), None),
        ),
        check_vma=False,
    )
```

profile of v0, /device:TPU:0, one launch (start us, length us, event | category | flops | bytes accessed | tf_op | source)
XLA Modules:
  0.0 518.4 jit_solution(5105015410426515977)
XLA Ops:
  23.4 4.1 collective-permute-done
  29.2 6.4 %collective-permute-done.1 = bf16[64,1536]{1,0:T(8,128)(2,1)} collective-permute-done((bf16[64,1536]{1,0:T(8,128)(2,1)S(1)}, bf16[64,1536]{1,0:T(8,128)(2,1)}, u32[]{:S(2)}, u32[]{:S(2)}) %collective-permute-start.1) | collective-permute-done | bytes 196640 | tf_op jit(solution)/shard_map/ppermute | solution.py:468
  40.2 9.2 %collective-permute-done.5 = bf16[64,1536]{1,0:T(8,128)(2,1)S(1)} collective-permute-done((bf16[64,1536]{1,0:T(8,128)(2,1)S(1)}, bf16[64,1536]{1,0:T(8,128)(2,1)S(1)}, u32[]{:S(2)}, u32[]{:S(2)}) %collective-permute-start.5) | collective-permute-done | bytes 196640 | tf_op jit(solution)/shard_map/ppermute | solution.py:468
  52.3 6.1 %all-to-all-start = ((bf16[8,32,384]{2,1,0:T(8,128)(2,1)}), bf16[8,32,384]{2,1,0:T(8,128)(2,1)S(1)}, u32[]{:S(2)}, u32[]{:S(2)}) async-start(bf16[8,32,384]{2,1,0:T(8,128)(2,1)} %copy.91), calls=%async_computation | async-start | bytes 393216 | tf_op jit(solution)/shard_map/all_to_all | solution.py:440
  58.5 5.3 %all-to-all-done = bf16[8,32,384]{2,1,0:T(8,128)(2,1)S(1)} async-done(((bf16[8,32,384]{2,1,0:T(8,128)(2,1)}), bf16[8,32,384]{2,1,0:T(8,128)(2,1)S(1)}, u32[]{:S(2)}, u32[]{:S(2)}) %all-to-all-start) | async-done | bytes 196640 | tf_op jit(solution)/shard_map/all_to_all | solution.py:440
  63.8 31.1 %all_to_all.85 = bf16[4,256,512]{2,1,0:T(8,128)(2,1)S(1)} all-to-all(bf16[4,256,512]{2,1,0:T(8,128)(2,1)S(1)} %broadcast_in_dim.132), channel_id=1, replica_groups=mesh['a'=4,'r'=2,'core'=2,'exp'=2] {'a'}, dimensions={0} | all-to-all | bytes 2097152 | tf_op jit(solution)/shard_map/all_to_all | solution.py:440
  109.1 17.0 %all-to-all-done.3 = bf16[4,128,1024]{2,1,0:T(8,128)(2,1)S(1)} async-done(((bf16[4,128,1024]{2,1,0:T(8,128)(2,1)}), bf16[4,128,1024]{2,1,0:T(8,128)(2,1)S(1)}, u32[]{:S(2)}, u32[]{:S(2)}) %all-to-all-start.3) | async-done | bytes 1048608 | tf_op jit(solution)/shard_map/all_to_all | solution.py:440
  127.6 4.8 all-to-all-start.4
  137.0 4.9 concatenate.23.table_ref
  144.0 10.9 %shard_map.392 = (bf16[1024,256]{1,0:T(8,128)(2,1)S(1)}, f32[1024,128]{1,0:T(8,128)S(1)}, bf16[8,128,128]{2,1,0:T(8,128)(2,1)S(1)}) custom-call(bf16[1024,1152]{1,0:T(8,128)(2,1)S(1)} %copy-done, bf16[1024,512]{1,0:T(8,128)(2,1)S(1)} %bitcast.154, f32[1024,256]{1,0:T(8,128)S(1)} %copy-done.2, f32[8,128,128]{2,1,0:T(8,128)S(1)} %and_convert_fusion.allow_ref), custom_call_target="tpu_custom_call" | custom-call | flops 805306368 | bytes 4980736 | tf_op jit(solution)/shard_map/pallas_call | solution.py:1085
  158.1 4.0 all-to-all-start.2
  175.6 4.3 all-to-all-start.5
  194.7 14.7 %all-to-all-done.5 = bf16[4,128,1152]{2,1,0:T(8,128)(2,1)} async-done(((bf16[4,128,1152]{2,1,0:T(8,128)(2,1)}), bf16[4,128,1152]{2,1,0:T(8,128)(2,1)}, u32[]{:S(2)}, u32[]{:S(2)}) %all-to-all-start.5) | async-done | bytes 1179680 | tf_op jit(solution)/shard_map/all_to_all | solution.py:440
  210.8 6.5 %all_to_all.86 = bf16[2,512,1152]{2,1,0:T(8,128)(2,1)} all-to-all(bf16[2,512,1152]{2,1,0:T(8,128)(2,1)S(1)} %broadcast_in_dim.138), channel_id=1, replica_groups=mesh['a'=4,'r'=2,'core'=2,'exp'=2] {'core'}, dimensions={0} | all-to-all | bytes 4718592 | tf_op jit(solution)/shard_map/all_to_all | solution.py:440
  221.8 9.7 %shard_map.394 = (bf16[1024,1024]{1,0:T(8,128)(2,1)S(1)}, f32[2,1024,1024]{2,1,0:T(8,128)S(1)}) custom-call(s32[1]{0:T(128)} %bitcast.10.place_ref, bf16[1024,1152]{1,0:T(8,128)(2,1)S(1)} %bitcast.157, bf16[2,1024,1536]{2,1,0:T(8,128)(2,1)S(1)} %bitcast.172), custom_call_target="tpu_custom_call" | custom-call | flops 6442450944 | bytes 23068672 | tf_op jit(solution)/shard_map/pallas_call | solution.py:526
  232.8 11.6 %shard_map.395 = (bf16[1024,1152]{1,0:T(8,128)(2,1)S(1)}, bf16[2,1024,1024]{2,1,0:T(8,128)(2,1)S(1)}, bf16[2,1024,512]{2,1,0:T(8,128)(2,1)S(1)}) custom-call(s32[1]{0:T(128)} %bitcast.10.place_ref, bf16[1024,1152]{1,0:T(8,128)(2,1)S(1)} %bitcast.158, bf16[1024,1024]{1,0:T(8,128)(2,1)S(1)} %bitcast.164, bf16[2,1024,1536]{2,1,0:T(8,128)(2,1)S(1)} %bitcast.173, ...), custom_call_target="tpu_custom_call" | custom-call | flops 6442450944 | bytes 27262976 | tf_op jit(solution)/shard_map/pallas_call | solution.py:550
  245.8 5.6 %all_to_all.87 = bf16[2,512,1152]{2,1,0:T(8,128)(2,1)S(1)} all-to-all(bf16[2,512,1152]{2,1,0:T(8,128)(2,1)S(1)} %bitcast.161), channel_id=1, replica_groups=mesh['a'=4,'r'=2,'core'=2,'exp'=2] {'core'}, dimensions={0} | all-to-all | bytes 4718592 | tf_op jit(solution)/shard_map/all_to_all | solution.py:440
  252.7 4.3 all-to-all-start.8
  266.5 12.4 %shard_map.396 = (bf16[512,1536]{1,0:T(8,128)(2,1)S(1)}, bf16[512,1536]{1,0:T(8,128)(2,1)}, bf16[512,1536]{1,0:T(8,128)(2,1)}, bf16[512,1536]{1,0:T(8,128)(2,1)}) custom-call(s32[8]{0:T(128)S(1)} %stack.39.where_ref, bf16[1024,1152]{1,0:T(8,128)(2,1)S(1)} %bitcast.159, bf16[2,1024,1024]{2,1,0:T(8,128)(2,1)S(1)} %copy-done.53, ...), custom_call_target="tpu_custom_call" | custom-call | flops 6442450944 | bytes 27262976 | tf_op jit(solution)/shard_map/pallas_call | solution.py:587
  286.2 4.3 all-to-all-start.9
  296.4 5.8 %shard_map.397 = (f32[128,1024]{1,0:T(8,128)S(1)}, bf16[8,128,128]{2,1,0:T(8,128)(2,1)S(1)}, bf16[1024,1152]{1,0:T(8,128)(2,1)S(1)}) custom-call(bf16[4,128,1152]{2,1,0:T(8,128)(2,1)} %all-to-all-done.8.refs_0_, bf16[1024,1024]{1,0:T(8,128)(2,1)S(1)} %copy-done.4, bf16[128,1024]{1,0:T(8,128)(2,1)S(1)} %copy-done.38, f32[128,1152]{1,0:T(8,128)S(1)} %copy-done.27, ...), custom_call_target="tpu_custom_call" | custom-call | flops 1 | bytes 1 | tf_op jit(solution)/shard_map/pallas_call | solution.py:418
  305.1 10.9 %all-to-all-done.9 = bf16[4,128,1024]{2,1,0:T(8,128)(2,1)} async-done(((bf16[4,128,1024]{2,1,0:T(8,128)(2,1)}), bf16[4,128,1024]{2,1,0:T(8,128)(2,1)}, u32[]{:S(2)}, u32[]{:S(2)}) %all-to-all-start.9) | async-done | bytes 1048608 | tf_op jit(solution)/shard_map/all_to_all | solution.py:440
  316.0 9.3 %all_to_all.88.mid_ref = bf16[8,128,128]{2,1,0:T(8,128)(2,1)S(1)} all-to-all(bf16[8,128,128]{2,1,0:T(8,128)(2,1)} %copy-done.42), channel_id=1, replica_groups=mesh['a'=4,'r'=2,'core'=2,'exp'=2] {'r','core','exp'}, dimensions={0} | all-to-all | bytes 524288 | tf_op jit(solution)/shard_map/all_to_all | solution.py:440
  331.3 11.6 %shard_map.398 = (bf16[1024,384]{1,0:T(8,128)(2,1)}, bf16[8,128,1024]{2,1,0:T(8,128)(2,1)}) custom-call(bf16[1024,1152]{1,0:T(8,128)(2,1)S(1)} %copy-done.1, bf16[1024,512]{1,0:T(8,128)(2,1)S(1)} %bitcast.155, f32[1024,256]{1,0:T(8,128)S(1)} %copy-done.3, f32[8,128,128]{2,1,0:T(8,128)S(1)} %copy-done.10, bf16[1024,256]{1,0:T(8,128)(2,1)S(1)} %copy-done.30, ...), custom_call_target="tpu_custom_call" | custom-call | flops 1610612736 | bytes 6291456 | tf_op jit(solution)/shard_map/pallas_call | solution.py:1085
  349.6 4.9 all-to-all-start.14
  366.9 9.8 %all-to-all-done.13 = bf16[4,128,1024]{2,1,0:T(8,128)(2,1)S(1)} async-done(((bf16[4,128,1024]{2,1,0:T(8,128)(2,1)}), bf16[4,128,1024]{2,1,0:T(8,128)(2,1)S(1)}, u32[]{:S(2)}, u32[]{:S(2)}) %all-to-all-start.13) | async-done | bytes 1048608 | tf_op jit(solution)/shard_map/all_to_all | solution.py:440
  390.1 27.9 %collective-permute-done.12 = bf16[512,1536]{1,0:T(8,128)(2,1)} collective-permute-done((bf16[512,1536]{1,0:T(8,128)(2,1)}, bf16[512,1536]{1,0:T(8,128)(2,1)}, u32[]{:S(2)}, u32[]{:S(2)}) %collective-permute-start.12) | collective-permute-done | bytes 1572896 | tf_op jit(solution)/shard_map/ppermute | solution.py:468
  417.9 31.7 %collective-permute-done.13 = bf16[512,1536]{1,0:T(8,128)(2,1)} collective-permute-done((bf16[512,1536]{1,0:T(8,128)(2,1)}, bf16[512,1536]{1,0:T(8,128)(2,1)}, u32[]{:S(2)}, u32[]{:S(2)}) %collective-permute-start.13) | collective-permute-done | bytes 1572896 | tf_op jit(solution)/shard_map/ppermute | solution.py:468
  461.0 4.3 all-to-all-start.15
  478.0 10.1 %collective-permute-done.20 = bf16[64,1536]{1,0:T(8,128)(2,1)S(1)} collective-permute-done((bf16[64,1536]{1,0:T(8,128)(2,1)S(1)}, bf16[64,1536]{1,0:T(8,128)(2,1)S(1)}, u32[]{:S(2)}, u32[]{:S(2)}) %collective-permute-start.20) | collective-permute-done | bytes 196640 | tf_op jit(solution)/shard_map/ppermute | solution.py:468
  492.3 6.4 %all-to-all-start.16 = ((bf16[4,32,1152]{2,1,0:T(8,128)(2,1)}), bf16[4,32,1152]{2,1,0:T(8,128)(2,1)S(1)}, u32[]{:S(2)}, u32[]{:S(2)}) async-start(bf16[4,32,1152]{2,1,0:T(8,128)(2,1)} %bitcast.62), calls=%async_computation.16 | async-start | bytes 589824 | tf_op jit(solution)/shard_map/all_to_all | solution.py:440
  498.7 7.7 %multiply_subtract_fusion = (f32[8,64,1024]{2,1,0:T(8,128)}, f32[8,64,1024]{2,1,0:T(8,128)}, f32[8,64,1024]{2,1,0:T(8,128)}) fusion(f32[8,64,1024]{2,1,0:T(8,128)} %param.41, f32[8,64,1536]{2,1,0:T(8,128)} %convert_element_type.271, f32[8,64,1024]{2,1,0:T(8,128)} %param.42, f32[8,64,1024]{2,1,0:T(8,128)} %param.43), kind=kLoop, calls=%fused_computation.33 | loop fusion | flops 7864320 | bytes 14680064 | tf_op jit(solution)/shard_map/sub | solution.py:62
  (294 shorter events, 185.9 us)
Async XLA Ops:
  7.2 125.3 %all-gather.3.cloned.1.call-start = ((), (), s32[]{:S(2)}) async-start(), calls=%async_computation.17 | async-start | bytes 2654208 | tf_op jit(solution)/shard_map/all_gather | solution.py:1139
  11.2 206.1 %all-gather.5.cloned.1.call-start = ((), (), s32[]{:S(2)}) async-start(), calls=%async_computation.18 | async-start | bytes 7864320 | tf_op jit(solution)/shard_map/all_gather | solution.py:1177
  15.3 12.3 %collective-permute-start = (bf16[64,1536]{1,0:T(8,128)(2,1)S(1)}, bf16[64,1536]{1,0:T(8,128)(2,1)}, u32[]{:S(2)}, u32[]{:S(2)}) collective-permute-start(bf16[64,1536]{1,0:T(8,128)(2,1)S(1)} %get-tuple-element.136), channel_id=1, source_target_pairs={{0,8},{2,10},{8,0},{10,2},{16,24},{18,26},{24,16},{26,18},{1,9},{3... | collective-permute-start | bytes 589832 | tf_op jit(solution)/shard_map/ppermute | solution.py:468
  18.3 17.3 %collective-permute-start.1 = (bf16[64,1536]{1,0:T(8,128)(2,1)S(1)}, bf16[64,1536]{1,0:T(8,128)(2,1)}, u32[]{:S(2)}, u32[]{:S(2)}) collective-permute-start(bf16[64,1536]{1,0:T(8,128)(2,1)S(1)} %get-tuple-element.137), channel_id=1, source_target_pairs={{0,16},{2,18},{8,24},{10,26},{16,0},{18,2},{24,8},{26,10},{1,17},{... | collective-permute-start | bytes 589832 | tf_op jit(solution)/shard_map/ppermute | solution.py:468
  20.8 16.4 %collective-permute-start.2 = (bf16[64,1536]{1,0:T(8,128)(2,1)S(1)}, bf16[64,1536]{1,0:T(8,128)(2,1)}, u32[]{:S(2)}, u32[]{:S(2)}) collective-permute-start(bf16[64,1536]{1,0:T(8,128)(2,1)S(1)} %get-tuple-element.138), channel_id=1, source_target_pairs={{0,24},{2,26},{8,16},{10,18},{16,8},{18,10},{24,0},{26,2},{1,25},{... | collective-permute-start | bytes 589832 | tf_op jit(solution)/shard_map/ppermute | solution.py:468
  20.8 18.0 %collective-permute-start.3 = (bf16[64,1536]{1,0:T(8,128)(2,1)S(1)}, bf16[64,1536]{1,0:T(8,128)(2,1)S(1)}, u32[]{:S(2)}, u32[]{:S(2)}) collective-permute-start(bf16[64,1536]{1,0:T(8,128)(2,1)S(1)} %get-tuple-element.139), channel_id=1, source_target_pairs={{0,2},{2,0},{8,10},{10,8},{16,18},{18,16},{24,26},{26,24},{1,3},{3... | collective-permute-start | bytes 589832 | tf_op jit(solution)/shard_map/ppermute | solution.py:468
  20.9 18.6 %collective-permute-start.4 = (bf16[64,1536]{1,0:T(8,128)(2,1)S(1)}, bf16[64,1536]{1,0:T(8,128)(2,1)S(1)}, u32[]{:S(2)}, u32[]{:S(2)}) collective-permute-start(bf16[64,1536]{1,0:T(8,128)(2,1)S(1)} %get-tuple-element.141), channel_id=1, source_target_pairs={{0,10},{2,8},{8,2},{10,0},{16,26},{18,24},{24,18},{26,16},{1,11},{... | collective-permute-start | bytes 589832 | tf_op jit(solution)/shard_map/ppermute | solution.py:468
  27.5 21.9 %collective-permute-start.5 = (bf16[64,1536]{1,0:T(8,128)(2,1)S(1)}, bf16[64,1536]{1,0:T(8,128)(2,1)S(1)}, u32[]{:S(2)}, u32[]{:S(2)}) collective-permute-start(bf16[64,1536]{1,0:T(8,128)(2,1)S(1)} %get-tuple-element.140), channel_id=1, source_target_pairs={{0,18},{2,16},{8,26},{10,24},{16,2},{18,0},{24,10},{26,8},{1,19},{... | collective-permute-start | bytes 589832 | tf_op jit(solution)/shard_map/ppermute | solution.py:468
  35.6 14.5 %collective-permute-start.6 = (bf16[64,1536]{1,0:T(8,128)(2,1)S(1)}, bf16[64,1536]{1,0:T(8,128)(2,1)S(1)}, u32[]{:S(2)}, u32[]{:S(2)}) collective-permute-start(bf16[64,1536]{1,0:T(8,128)(2,1)S(1)} %get-tuple-element.134), channel_id=1, source_target_pairs={{0,26},{2,24},{8,18},{10,16},{16,10},{18,8},{24,2},{26,0},{1,27},{... | collective-permute-start | bytes 589832 | tf_op jit(solution)/shard_map/ppermute | solution.py:468
  96.9 29.1 %all-to-all-start.3 = ((bf16[4,128,1024]{2,1,0:T(8,128)(2,1)}), bf16[4,128,1024]{2,1,0:T(8,128)(2,1)S(1)}, u32[]{:S(2)}, u32[]{:S(2)}) async-start(bf16[4,128,1024]{2,1,0:T(8,128)(2,1)} %broadcast_in_dim.134), calls=%async_computation.3 | async-start | bytes 2097152 | tf_op jit(solution)/shard_map/all_to_all | solution.py:440
  104.7 75.2 %collective-permute-start.7 = (bf16[128,1024]{0,1:T(8,128)(2,1)}, bf16[128,1024]{0,1:T(8,128)(2,1)}, u32[]{:S(2)}, u32[]{:S(2)}) collective-permute-start(bf16[128,1024]{0,1:T(8,128)(2,1)} %fusion.19), channel_id=1, source_target_pairs={{0,8},{8,0},{16,24},{24,16},{1,9},{9,1},{17,25},{25,17},{2,10},{10... | collective-permute-start | bytes 786440 | tf_op jit(solution)/shard_map/ppermute | solution.py:468
  104.9 76.7 %collective-permute-start.8 = (bf16[128,1024]{0,1:T(8,128)(2,1)}, bf16[128,1024]{0,1:T(8,128)(2,1)}, u32[]{:S(2)}, u32[]{:S(2)}) collective-permute-start(bf16[128,1024]{0,1:T(8,128)(2,1)} %fusion.19), channel_id=1, source_target_pairs={{0,16},{8,24},{16,0},{24,8},{1,17},{9,25},{17,1},{25,9},{2,18},{10... | collective-permute-start | bytes 786440 | tf_op jit(solution)/shard_map/ppermute | solution.py:468
  106.7 78.8 %collective-permute-start.9 = (bf16[128,1024]{0,1:T(8,128)(2,1)}, bf16[128,1024]{0,1:T(8,128)(2,1)}, u32[]{:S(2)}, u32[]{:S(2)}) collective-permute-start(bf16[128,1024]{0,1:T(8,128)(2,1)} %fusion.19), channel_id=1, source_target_pairs={{0,24},{8,16},{16,8},{24,0},{1,25},{9,17},{17,9},{25,1},{2,26},{10... | collective-permute-start | bytes 786440 | tf_op jit(solution)/shard_map/ppermute | solution.py:468
  127.6 30.4 %all-to-all-start.4 = ((bf16[2,512,1024]{2,1,0:T(8,128)(2,1)}), bf16[2,512,1024]{2,1,0:T(8,128)(2,1)}, u32[]{:S(2)}, u32[]{:S(2)}) async-start(bf16[2,512,1024]{2,1,0:T(8,128)(2,1)} %broadcast_in_dim.136), calls=%async_computation.4 | async-start | bytes 4194304 | tf_op jit(solution)/shard_map/all_to_all | solution.py:440
  175.6 33.7 %all-to-all-start.5 = ((bf16[4,128,1152]{2,1,0:T(8,128)(2,1)}), bf16[4,128,1152]{2,1,0:T(8,128)(2,1)}, u32[]{:S(2)}, u32[]{:S(2)}) async-start(bf16[4,128,1152]{2,1,0:T(8,128)(2,1)} %copy-done.23), calls=%async_computation.5 | async-start | bytes 2359296 | tf_op jit(solution)/shard_map/all_to_all | solution.py:440
  252.7 33.4 %all-to-all-start.8 = ((bf16[4,128,1152]{2,1,0:T(8,128)(2,1)}), bf16[4,128,1152]{2,1,0:T(8,128)(2,1)}, u32[]{:S(2)}, u32[]{:S(2)}) async-start(bf16[4,128,1152]{2,1,0:T(8,128)(2,1)} %bitcast.175), calls=%async_computation.8 | async-start | bytes 2359296 | tf_op jit(solution)/shard_map/all_to_all | solution.py:440
  259.3 20.9 %collective-permute-start.11 = (bf16[512,1024]{1,0:T(8,128)(2,1)}, bf16[512,1024]{1,0:T(8,128)(2,1)}, u32[]{:S(2)}, u32[]{:S(2)}) collective-permute-start(bf16[512,1024]{1,0:T(8,128)(2,1)} %dynamic-slice_bitcast_fusion), channel_id=1, source_target_pairs={{0,2},{2,0},{1,3},{3,1},{4,6},{6,4},{5,7},{7,5},{8,10},{10,8},{9,1... | collective-permute-start | bytes 3145736 | tf_op jit(solution)/shard_map/ppermute | solution.py:468
  286.2 29.8 %all-to-all-start.9 = ((bf16[4,128,1024]{2,1,0:T(8,128)(2,1)}), bf16[4,128,1024]{2,1,0:T(8,128)(2,1)}, u32[]{:S(2)}, u32[]{:S(2)}) async-start(bf16[4,128,1024]{2,1,0:T(8,128)(2,1)} %bitcast.181), calls=%async_computation.9 | async-start | bytes 2097152 | tf_op jit(solution)/shard_map/all_to_all | solution.py:440
  357.7 19.1 %all-to-all-start.13 = ((bf16[4,128,1024]{2,1,0:T(8,128)(2,1)}), bf16[4,128,1024]{2,1,0:T(8,128)(2,1)S(1)}, u32[]{:S(2)}, u32[]{:S(2)}) async-start(bf16[4,128,1024]{2,1,0:T(8,128)(2,1)} %bitcast.178), calls=%async_computation.13 | async-start | bytes 2097152 | tf_op jit(solution)/shard_map/all_to_all | solution.py:440
  361.4 56.5 %collective-permute-start.12 = (bf16[512,1536]{1,0:T(8,128)(2,1)}, bf16[512,1536]{1,0:T(8,128)(2,1)}, u32[]{:S(2)}, u32[]{:S(2)}) collective-permute-start(bf16[512,1536]{1,0:T(8,128)(2,1)} %get-tuple-element.92), channel_id=1, source_target_pairs={{0,5},{1,4},{4,1},{5,0},{2,7},{3,6},{6,3},{7,2},{8,13},{9,12},{12,... | collective-permute-start | bytes 4718600 | tf_op jit(solution)/shard_map/ppermute | solution.py:468
  364.4 85.3 %collective-permute-start.13 = (bf16[512,1536]{1,0:T(8,128)(2,1)}, bf16[512,1536]{1,0:T(8,128)(2,1)}, u32[]{:S(2)}, u32[]{:S(2)}) collective-permute-start(bf16[512,1536]{1,0:T(8,128)(2,1)} %get-tuple-element.93), channel_id=1, source_target_pairs={{0,1},{1,0},{4,5},{5,4},{2,3},{3,2},{6,7},{7,6},{8,9},{9,8},{12,13... | collective-permute-start | bytes 4718600 | tf_op jit(solution)/shard_map/ppermute | solution.py:468
  364.9 85.5 %collective-permute-start.14 = (bf16[512,1536]{1,0:T(8,128)(2,1)}, bf16[512,1536]{1,0:T(8,128)(2,1)}, u32[]{:S(2)}, u32[]{:S(2)}) collective-permute-start(bf16[512,1536]{1,0:T(8,128)(2,1)} %get-tuple-element.94), channel_id=1, source_target_pairs={{0,4},{1,5},{4,0},{5,1},{2,6},{3,7},{6,2},{7,3},{8,12},{9,13},{12,... | collective-permute-start | bytes 4718600 | tf_op jit(solution)/shard_map/ppermute | solution.py:468
  376.8 75.5 %all-to-all-start.11 = ((bf16[32,32,384]{2,1,0:T(8,128)(2,1)}), bf16[32,32,384]{2,1,0:T(8,128)(2,1)S(1)}, u32[]{:S(2)}, u32[]{:S(2)}) async-start(bf16[32,32,384]{2,1,0:T(8,128)(2,1)} %bitcast.55), calls=%async_computation.11 | async-start | bytes 1572864 | tf_op jit(solution)/shard_map/all_to_all | solution.py:440
  456.6 11.9 %collective-permute-start.15 = (bf16[64,1536]{1,0:T(8,128)(2,1)}, bf16[64,1536]{1,0:T(8,128)(2,1)}, u32[]{:S(2)}, u32[]{:S(2)}) collective-permute-start(bf16[64,1536]{1,0:T(8,128)(2,1)} %get-tuple-element.132), channel_id=1, source_target_pairs={{0,8},{2,10},{8,0},{10,2},{16,24},{18,26},{24,16},{26,18},{1,9},{3... | collective-permute-start | bytes 589832 | tf_op jit(solution)/shard_map/ppermute | solution.py:468
  456.6 17.5 %collective-permute-start.16 = (bf16[64,1536]{1,0:T(8,128)(2,1)}, bf16[64,1536]{1,0:T(8,128)(2,1)}, u32[]{:S(2)}, u32[]{:S(2)}) collective-permute-start(bf16[64,1536]{1,0:T(8,128)(2,1)} %get-tuple-element.131), channel_id=1, source_target_pairs={{0,16},{2,18},{8,24},{10,26},{16,0},{18,2},{24,8},{26,10},{1,17},{... | collective-permute-start | bytes 589832 | tf_op jit(solution)/shard_map/ppermute | solution.py:468
  458.7 16.4 %collective-permute-start.17 = (bf16[64,1536]{1,0:T(8,128)(2,1)}, bf16[64,1536]{1,0:T(8,128)(2,1)}, u32[]{:S(2)}, u32[]{:S(2)}) collective-permute-start(bf16[64,1536]{1,0:T(8,128)(2,1)} %get-tuple-element.130), channel_id=1, source_target_pairs={{0,24},{2,26},{8,16},{10,18},{16,8},{18,10},{24,0},{26,2},{1,25},{... | collective-permute-start | bytes 589832 | tf_op jit(solution)/shard_map/ppermute | solution.py:468
  461.0 15.1 %collective-permute-start.18 = (bf16[64,1536]{1,0:T(8,128)(2,1)}, bf16[64,1536]{1,0:T(8,128)(2,1)}, u32[]{:S(2)}, u32[]{:S(2)}) collective-permute-start(bf16[64,1536]{1,0:T(8,128)(2,1)} %get-tuple-element.129), channel_id=1, source_target_pairs={{0,2},{2,0},{8,10},{10,8},{16,18},{18,16},{24,26},{26,24},{1,3},{3... | collective-permute-start | bytes 589832 | tf_op jit(solution)/shard_map/ppermute | solution.py:468
  461.0 16.0 %collective-permute-start.19 = (bf16[64,1536]{1,0:T(8,128)(2,1)}, bf16[64,1536]{1,0:T(8,128)(2,1)}, u32[]{:S(2)}, u32[]{:S(2)}) collective-permute-start(bf16[64,1536]{1,0:T(8,128)(2,1)} %get-tuple-element.128), channel_id=1, source_target_pairs={{0,10},{2,8},{8,2},{10,0},{16,26},{18,24},{24,18},{26,16},{1,11},{... | collective-permute-start | bytes 589832 | tf_op jit(solution)/shard_map/ppermute | solution.py:468
  461.0 29.2 %all-to-all-start.15 = ((bf16[4,128,1152]{2,1,0:T(8,128)(2,1)}), bf16[4,128,1152]{2,1,0:T(8,128)(2,1)}, u32[]{:S(2)}, u32[]{:S(2)}) async-start(bf16[4,128,1152]{2,1,0:T(8,128)(2,1)} %bitcast.176), calls=%async_computation.15 | async-start | bytes 2359296 | tf_op jit(solution)/shard_map/all_to_all | solution.py:440
  468.6 19.5 %collective-permute-start.20 = (bf16[64,1536]{1,0:T(8,128)(2,1)S(1)}, bf16[64,1536]{1,0:T(8,128)(2,1)S(1)}, u32[]{:S(2)}, u32[]{:S(2)}) collective-permute-start(bf16[64,1536]{1,0:T(8,128)(2,1)S(1)} %copy-done.64), channel_id=1, source_target_pairs={{0,18},{2,16},{8,26},{10,24},{16,2},{18,0},{24,10},{26,8},{1,19},{... | collective-permute-start | bytes 589832 | tf_op jit(solution)/shard_map/ppermute | solution.py:468
  474.2 13.9 %collective-permute-start.21 = (bf16[64,1536]{1,0:T(8,128)(2,1)S(1)}, bf16[64,1536]{1,0:T(8,128)(2,1)S(1)}, u32[]{:S(2)}, u32[]{:S(2)}) collective-permute-start(bf16[64,1536]{1,0:T(8,128)(2,1)S(1)} %get-tuple-element.126), channel_id=1, source_target_pairs={{0,26},{2,24},{8,18},{10,16},{16,10},{18,8},{24,2},{26,0},{1,27},{... | collective-permute-start | bytes 589832 | tf_op jit(solution)/shard_map/ppermute | solution.py:468
  492.3 17.8 %all-to-all-start.16 = ((bf16[4,32,1152]{2,1,0:T(8,128)(2,1)}), bf16[4,32,1152]{2,1,0:T(8,128)(2,1)S(1)}, u32[]{:S(2)}, u32[]{:S(2)}) async-start(bf16[4,32,1152]{2,1,0:T(8,128)(2,1)} %bitcast.62), calls=%async_computation.16 | async-start | bytes 589824 | tf_op jit(solution)/shard_map/all_to_all | solution.py:440
  (74 other events, 381.7 us)
Sparse Core Ops, SparseCore 0:
  11.3 31.6 all-gather.2
  50.9 85.0 all-gather.4
where the time goes:
time: 522 us; the launch traced here: 518 us
  waiting for transfers between devices  164 us (31%)
  local copies, waits for them, and re-layouts  88.1 us (17%)
  starting transfers between devices  78.2 us (15%)
  Pallas kernels  65.6 us (13%)
  blocking collectives  52.6 us (10%)
  other arithmetic  44.9 us (9%)
  between operations  15 us (3%)
  matrix products  9.96 us (2%)
    ppermute x22, waiting for transfers between devices, partner(): return lax.ppermute(values, names, pairs)  94.3 us
    all_to_all x13, waiting for transfers between devices, exchange(): return lax.all_to_all(values, axes, split_axis=0, concat_axis=0, tiled=True)  69.6 us
    all_to_all x13, starting transfers between devices, exchange(): return lax.all_to_all(values, axes, split_axis=0, concat_axis=0, tiled=True)  56.7 us
    all_to_all x4, blocking collectives, exchange(): return lax.all_to_all(values, axes, split_axis=0, concat_axis=0, tiled=True)  52.6 us
    unnamed x141, local copies, waits for them, and re-layouts  42.4 us
    pallas_call x2, Pallas kernels, block_call(): pl.pallas_call(kernel, grid=(blocks,), out_shape=[item for item, _, _ in...  22.5 us
    dynamic_update_slice x21, local copies, waits for them, and re-layouts, in_order(): result = lax.dynamic_update_index_in_dim(result, part, me ^ step, 0)  22.1 us
    ppermute x22, starting transfers between devices, partner(): return lax.ppermute(values, names, pairs)  21.3 us
  transfers between devices with their start and end apart: 37, of which 19 were waited for; matrix products, arithmetic and copies ran while one was open for 17% of the time, Pallas kernels for 6%

commit v1 on v0

--- a/solution.py
+++ b/solution.py
@@ -1160,23 +1160,12 @@
         axis=2,
     )
     pack = exchange(pack.transpose(1, 0, 2), plane).reshape(lines, 3 * LANES)
+    expert_pack = jnp.concatenate([in_weight.astype(bf16), down_weight.astype(bf16)], axis=2)
+    pieces = pieces_for(expert_pack, ("core", "a"))
+    pack, *pieces = lax.optimization_barrier((pack, *pieces))
     pack = jnp.concatenate([pack, out_weight.astype(bf16).reshape(lines, LANES)], axis=1)
     pack = spread(pack, "a")
-    out_full = pack[:, 3 * LANES :].reshape(n_a * local_rows, width)
-    out_full = spread(spread(out_full, ("r", "exp")), "core")
-    out_full = out_full.reshape(n_c, n_r, n_e, n_a, local_rows, width)
-    out_full = out_full.transpose(3, 1, 0, 2, 4, 5).reshape(width, width)
-    extra_full = pack[:, 2 * LANES : 3 * LANES]
-    first_gain = extra_full[:, experts].astype(f32)
-
-    expert_pack = jnp.concatenate([in_weight.astype(bf16), down_weight.astype(bf16)], axis=2)
-    expert_pack = exchange_aside(pieces_for(expert_pack, ("core", "a")), ("core", "a"))
-    cot_expert = dot_nn(cotangent, reorder_matrix(home, expert)).astype(bf16)
-    cot_expert, expert_pack = lax.optimization_barrier((cot_expert, expert_pack))
-    cot_group = spread_aside(spread_aside(cot_expert, "a"), "core")
-    expert_full = lax.all_gather(expert_pack, ("exp", "r"), axis=0, tiled=True).reshape(
-        n_e, width, 3 * FF
-    )
+    expert_pack = exchange_aside(pieces, ("core", "a"))
 
     cosine, sine = rope_tables(x_all[:, width].astype(f32), HEAD_DIMENSION)
     repeat = LANES // HEAD_DIMENSION
@@ -1190,6 +1179,20 @@
     used = jnp.any(
         routes[:, :, None] == jnp.arange(LANES, dtype=jnp.int32)[None, None, :], axis=1
     ).astype(f32)
+
+    cot_expert = dot_nn(cotangent, reorder_matrix(home, expert)).astype(bf16)
+    to_expert = reorder_matrix(home, expert)
+    pack, expert_pack, tables, allowed, used, cot_expert, to_expert = lax.optimization_barrier(
+        (pack, expert_pack, tables, allowed, used, cot_expert, to_expert)
+    )
+    out_rows = pack[:, 3 * LANES :].reshape(n_a * local_rows, width)
+    out_rows = spread(out_rows, ("r", "exp"))
+    extra_full = pack[:, 2 * LANES : 3 * LANES]
+    first_gain = extra_full[:, experts].astype(f32)
+    cot_group = spread_aside(spread_aside(cot_expert, "a"), "core")
+    expert_full = lax.all_gather(expert_pack, ("exp", "r"), axis=0, tiled=True).reshape(
+        n_e, width, 3 * FF
+    )
 
     def same(index):
         return index
@@ -1213,11 +1216,15 @@
         [],
         flops=2 * places * rows * width * 3 * LANES,
     )
+    attended, out_rows = lax.optimization_barrier((attended, out_rows))
     attended = exchange(attended, plane)
+    attended, out_rows = lax.optimization_barrier((attended, out_rows))
+    out_full = spread(out_rows, "core").reshape(n_c, n_r, n_e, n_a, local_rows, width)
+    out_full = out_full.transpose(3, 1, 0, 2, 4, 5).reshape(width, width)
     wide, sent = whole_call(
         functools.partial(home_forward, experts, n_a),
         [shape((rows, width + LANES), f32), shape((n_a, rows, width + LANES), bf16)],
-        [tokens, attended, out_full, extra_full, used, reorder_matrix(home, expert)],
+        [tokens, attended, out_full, extra_full, used, to_expert],
         flops=4 * rows * width * width,
     )
 
@@ -1261,6 +1268,11 @@
     )
     mid, out = lax.optimization_barrier((mid, out))
     mid = exchange(mid, plane)
+    mid, out_grad = lax.optimization_barrier((mid, out_grad))
+    out_grad = collect(out_grad, "core").astype(bf16)
+    out_grad = collect(out_grad, ("r", "exp")).astype(bf16)
+    out_grad = exchange(out_grad.reshape(n_a, local_rows, query_width + LANES), "a")
+    mid, out_grad, *received = lax.optimization_barrier((mid, out_grad, *received))
 
     def core_first(index):
         return (index // n_e % n_c * n_r + index // (n_c * n_e)) * n_e + index % n_e
@@ -1282,16 +1294,19 @@
         ],
         flops=2 * places * rows * width * 6 * LANES,
     )
-    qkv_grad, out_grad = lax.optimization_barrier((qkv_grad, out_grad))
     qkv_grad = exchange(qkv_grad.reshape(n_a * places, local_rows, 3 * LANES), MESH_AXES)
     normed_grad = collect(normed_grad.reshape(places * rows, width), "core").astype(bf16)
+    expert_grad = received[0].astype(f32)
+    for part in received[1:]:
+        expert_grad = expert_grad + part.astype(f32)
+    expert_grad = expert_grad.astype(bf16).reshape(
+        n_c * n_a, width // (n_r * n_c * n_a), 3 * FF
+    )
+    expert_grad = exchange_aside(
+        pieces_for(expert_grad, ("core", "a")), ("core", "a")
+    ).astype(f32)
+    normed_grad, expert_grad = lax.optimization_barrier((normed_grad, expert_grad))
     normed_grad = collect(normed_grad, ("r", "exp"))
-    out_grad = collect(out_grad, "core").astype(bf16)
-    qkv_grad, normed_grad, out_grad, *received = lax.optimization_barrier(
-        (qkv_grad, normed_grad, out_grad, *received)
-    )
-    out_grad = collect(out_grad, ("r", "exp")).astype(bf16)
-    out_grad = exchange(out_grad.reshape(n_a, local_rows, query_width + LANES), "a")
 
     residual = tokens.astype(f32)
     first_scale = rms_scale(residual)
@@ -1306,15 +1321,6 @@
         mixed = mixed + dot_nn(out[index], from_expert)
     block_out = (wide[:, :width] + mixed).astype(bf16)
 
-    expert_grad = received[0].astype(f32)
-    for part in received[1:]:
-        expert_grad = expert_grad + part.astype(f32)
-    expert_grad = expert_grad.astype(bf16).reshape(
-        n_c * n_a, width // (n_r * n_c * n_a), 3 * FF
-    )
-    expert_grad = exchange_aside(
-        pieces_for(expert_grad, ("core", "a")), ("core", "a")
-    ).astype(f32)
     d_in = expert_grad[:, :, : 2 * FF]
     d_down = expert_grad[:, :, 2 * FF :]
 

time: 522 us -> 501 us (0.960)
  local copies, waits for them, and re-layouts: 88.1 us -> 72.8 us
  blocking collectives: 52.6 us -> 39.9 us
  waiting for transfers between devices: 164 us -> 173 us
    ppermute x22, waiting for transfers between devices: 94.3 us -> 109 us  [partner(): return lax.ppermute(values, names, pairs)]
    all_to_all x4 -> x6, blocking collectives: 52.6 us -> 39.9 us  [exchange(): return lax.all_to_all(values, axes, split_axis=0, concat_axis=0, tiled=True)]
    dynamic_update_slice x21 -> x22, local copies, waits for them, and re-layouts: 22.1 us -> 14.6 us  [in_order(): result = lax.dynamic_update_index_in_dim(result, part, me ^ step, 0)]
    ppermute x22, starting transfers between devices: 21.3 us -> 27.2 us  [partner(): return lax.ppermute(values, names, pairs)]
    unnamed x141 -> x159, local copies, waits for them, and re-layouts: 42.4 us -> 36.7 us
    all_to_all x13 -> x11, waiting for transfers between devices: 69.6 us -> 64.5 us  [exchange(): return lax.all_to_all(values, axes, split_axis=0, concat_axis=0, tiled=True)]
    all_to_all x13 -> x11, starting transfers between devices: 56.7 us -> 51.6 us  [exchange(): return lax.all_to_all(values, axes, split_axis=0, concat_axis=0, tiled=True)]
  transfers between devices with their start and end apart: 37 -> 35, of which waited for: 19 -> 15; matrix products, arithmetic and copies ran while one was open for 17% -> 16% of each run, Pallas kernels for 6% -> 8%
where the time goes in v1:
time: 501 us; the launch traced here: 498 us
  waiting for transfers between devices  173 us (35%)
  starting transfers between devices  78.9 us (16%)
  local copies, waits for them, and re-layouts  72.8 us (15%)
  Pallas kernels  64.3 us (13%)
  other arithmetic  42.7 us (9%)
  blocking collectives  39.9 us (8%)
  between operations  15.2 us (3%)
  matrix products  11 us (2%)
    ppermute x22, waiting for transfers between devices, partner(): return lax.ppermute(values, names, pairs)  109 us
    all_to_all x11, waiting for transfers between devices, exchange(): return lax.all_to_all(values, axes, split_axis=0, concat_axis=0, tiled=True)  64.5 us
    all_to_all x11, starting transfers between devices, exchange(): return lax.all_to_all(values, axes, split_axis=0, concat_axis=0, tiled=True)  51.6 us
    all_to_all x6, blocking collectives, exchange(): return lax.all_to_all(values, axes, split_axis=0, concat_axis=0, tiled=True)  39.9 us
    unnamed x159, local copies, waits for them, and re-layouts  36.7 us
    ppermute x22, starting transfers between devices, partner(): return lax.ppermute(values, names, pairs)  27.2 us
    pallas_call x2, Pallas kernels, block_call(): pl.pallas_call(kernel, grid=(blocks,), out_shape=[item for item, _, _ in...  22.2 us
    dynamic_update_slice x22, local copies, waits for them, and re-layouts, in_order(): result = lax.dynamic_update_index_in_dim(result, part, me ^ step, 0)  14.6 us
  transfers between devices with their start and end apart: 35, of which 15 were waited for; matrix products, arithmetic and copies ran while one was open for 16% of the time, Pallas kernels for 8%

profile of v1, /device:TPU:0, one launch (start us, length us, event | category | flops | bytes accessed | tf_op | source)
XLA Modules:
  0.0 497.9 jit_solution(10359981104948675917)
XLA Ops:
  11.1 5.2 %all-to-all-start = ((bf16[8,32,384]{2,1,0:T(8,128)(2,1)}), bf16[8,32,384]{2,1,0:T(8,128)(2,1)S(1)}, u32[]{:S(2)}, u32[]{:S(2)}) async-start(bf16[8,32,384]{2,1,0:T(8,128)(2,1)} %copy.91), calls=%async_computation | async-start | bytes 393216 | tf_op jit(solution)/shard_map/all_to_all | solution.py:440
  33.7 4.9 all-to-all-start.1
  41.7 4.7 collective-permute-done.1
  51.0 33.1 %collective-permute-done.5 = bf16[64,1536]{1,0:T(8,128)(2,1)S(1)} collective-permute-done((bf16[64,1536]{1,0:T(8,128)(2,1)S(1)}, bf16[64,1536]{1,0:T(8,128)(2,1)S(1)}, u32[]{:S(2)}, u32[]{:S(2)}) %collective-permute-start.5) | collective-permute-done | bytes 196640 | tf_op jit(solution)/shard_map/ppermute | solution.py:468
  89.1 4.9 concatenate.24.table_ref
  104.1 4.8 collective-permute-start.7
  113.7 10.9 %shard_map.392 = (bf16[1024,256]{1,0:T(8,128)(2,1)S(1)}, f32[1024,128]{1,0:T(8,128)S(1)}, bf16[8,128,128]{2,1,0:T(8,128)(2,1)S(1)}) custom-call(bf16[1024,1152]{1,0:T(8,128)(2,1)S(1)} %copy-done, bf16[1024,512]{1,0:T(8,128)(2,1)S(1)} %bitcast.162, f32[1024,256]{1,0:T(8,128)S(1)} %copy-done.2, f32[8,128,128]{2,1,0:T(8,128)S(1)} %copy-done.9), custom_call_target="tpu_custom_call" | custom-call | flops 805306368 | bytes 4980736 | tf_op jit(solution)/shard_map/pallas_call | solution.py:1085
  133.2 5.6 %all-to-all-done.3.refs_1_.refs_6_ = bf16[8,128,128]{2,1,0:T(8,128)(2,1)S(1)} async-done(((bf16[8,128,128]{2,1,0:T(8,128)(2,1)}), bf16[8,128,128]{2,1,0:T(8,128)(2,1)S(1)}, u32[]{:S(2)}, u32[]{:S(2)}) %all-to-all-start.3) | async-done | bytes 262176 | tf_op jit(solution)/shard_map/all_to_all | solution.py:440
  140.4 5.4 %all_to_all.85 = bf16[2,512,1024]{2,1,0:T(8,128)(2,1)S(1)} all-to-all(bf16[2,512,1024]{2,1,0:T(8,128)(2,1)S(1)} %broadcast_in_dim.144), channel_id=1, replica_groups=mesh['a'=4,'r'=2,'core'=2,'exp'=2] {'core'}, dimensions={0} | all-to-all | bytes 4194304 | tf_op jit(solution)/shard_map/all_to_all | solution.py:440
  150.7 7.6 %all-to-all-start.5 = ((bf16[4,128,1152]{2,1,0:T(8,128)(2,1)}), bf16[4,128,1152]{2,1,0:T(8,128)(2,1)}, u32[]{:S(2)}, u32[]{:S(2)}) async-start(bf16[4,128,1152]{2,1,0:T(8,128)(2,1)} %copy-done.27), calls=%async_computation.5 | async-start | bytes 2359296 | tf_op jit(solution)/shard_map/all_to_all | solution.py:440
  173.0 14.8 %all-to-all-done.5 = bf16[4,128,1152]{2,1,0:T(8,128)(2,1)} async-done(((bf16[4,128,1152]{2,1,0:T(8,128)(2,1)}), bf16[4,128,1152]{2,1,0:T(8,128)(2,1)}, u32[]{:S(2)}, u32[]{:S(2)}) %all-to-all-start.5) | async-done | bytes 1179680 | tf_op jit(solution)/shard_map/all_to_all | solution.py:440
  189.3 6.6 %all_to_all.86 = bf16[2,512,1152]{2,1,0:T(8,128)(2,1)} all-to-all(bf16[2,512,1152]{2,1,0:T(8,128)(2,1)S(1)} %broadcast_in_dim.146), channel_id=1, replica_groups=mesh['a'=4,'r'=2,'core'=2,'exp'=2] {'core'}, dimensions={0} | all-to-all | bytes 4718592 | tf_op jit(solution)/shard_map/all_to_all | solution.py:440
  200.3 9.7 %shard_map.394 = (bf16[1024,1024]{1,0:T(8,128)(2,1)S(1)}, f32[2,1024,1024]{2,1,0:T(8,128)S(1)}) custom-call(s32[1]{0:T(128)} %bitcast.27.place_ref, bf16[1024,1152]{1,0:T(8,128)(2,1)S(1)} %bitcast.165, bf16[2,1024,1536]{2,1,0:T(8,128)(2,1)S(1)} %bitcast.181), custom_call_target="tpu_custom_call" | custom-call | flops 6442450944 | bytes 23068672 | tf_op jit(solution)/shard_map/pallas_call | solution.py:526
  211.3 11.6 %shard_map.395 = (bf16[1024,1152]{1,0:T(8,128)(2,1)S(1)}, bf16[2,1024,1024]{2,1,0:T(8,128)(2,1)S(1)}, bf16[2,1024,512]{2,1,0:T(8,128)(2,1)S(1)}) custom-call(s32[1]{0:T(128)} %bitcast.27.place_ref, bf16[1024,1152]{1,0:T(8,128)(2,1)S(1)} %bitcast.166, bf16[1024,1024]{1,0:T(8,128)(2,1)S(1)} %bitcast.172, bf16[2,1024,1536]{2,1,0:T(8,128)(2,1)S(1)} %bitcast.182, ...), custom_call_target="tpu_custom_call" | custom-call | flops 6442450944 | bytes 27262976 | tf_op jit(solution)/shard_map/pallas_call | solution.py:550
  224.3 5.6 %all_to_all.87 = bf16[2,512,1152]{2,1,0:T(8,128)(2,1)S(1)} all-to-all(bf16[2,512,1152]{2,1,0:T(8,128)(2,1)S(1)} %bitcast.169), channel_id=1, replica_groups=mesh['a'=4,'r'=2,'core'=2,'exp'=2] {'core'}, dimensions={0} | all-to-all | bytes 4718592 | tf_op jit(solution)/shard_map/all_to_all | solution.py:440
  231.2 4.3 all-to-all-start.8
  245.0 12.4 %shard_map.396 = (bf16[512,1536]{1,0:T(8,128)(2,1)S(1)}, bf16[512,1536]{1,0:T(8,128)(2,1)}, bf16[512,1536]{1,0:T(8,128)(2,1)}, bf16[512,1536]{1,0:T(8,128)(2,1)}) custom-call(s32[8]{0:T(128)S(1)} %stack.39.where_ref, bf16[1024,1152]{1,0:T(8,128)(2,1)S(1)} %bitcast.167, bf16[2,1024,1024]{2,1,0:T(8,128)(2,1)S(1)} %copy-done.57, ...), custom_call_target="tpu_custom_call" | custom-call | flops 6442450944 | bytes 27262976 | tf_op jit(solution)/shard_map/pallas_call | solution.py:587
  264.7 4.3 all-to-all-start.9
  275.9 5.7 %shard_map.397 = (f32[128,1024]{1,0:T(8,128)S(1)}, bf16[8,128,128]{2,1,0:T(8,128)(2,1)S(1)}, bf16[1024,1152]{1,0:T(8,128)(2,1)S(1)}) custom-call(bf16[4,128,1152]{2,1,0:T(8,128)(2,1)} %all-to-all-done.8.refs_0_, bf16[1024,1024]{1,0:T(8,128)(2,1)S(1)} %copy-done.4, bf16[128,1024]{1,0:T(8,128)(2,1)S(1)} %copy-done.42, f32[128,1152]{1,0:T(8,128)S(1)} %copy-done.31, ...), custom_call_target="tpu_custom_call" | custom-call | flops 1 | bytes 1 | tf_op jit(solution)/shard_map/pallas_call | solution.py:418
  284.5 10.0 %all-to-all-done.9 = bf16[4,128,1024]{2,1,0:T(8,128)(2,1)} async-done(((bf16[4,128,1024]{2,1,0:T(8,128)(2,1)}), bf16[4,128,1024]{2,1,0:T(8,128)(2,1)}, u32[]{:S(2)}, u32[]{:S(2)}) %all-to-all-start.9) | async-done | bytes 1048608 | tf_op jit(solution)/shard_map/all_to_all | solution.py:440
  294.5 10.1 %all_to_all.88.mid_ref = bf16[8,128,128]{2,1,0:T(8,128)(2,1)} all-to-all(bf16[8,128,128]{2,1,0:T(8,128)(2,1)} %copy-done.46), channel_id=1, replica_groups=mesh['a'=4,'r'=2,'core'=2,'exp'=2] {'r','core','exp'}, dimensions={0} | all-to-all | bytes 524288 | tf_op jit(solution)/shard_map/all_to_all | solution.py:440
  304.6 6.8 %all_to_all.89 = bf16[2,512,1152]{2,1,0:T(8,128)(2,1)S(1)} all-to-all(bf16[2,512,1152]{2,1,0:T(8,128)(2,1)} %bitcast.168), channel_id=1, replica_groups=mesh['a'=4,'r'=2,'core'=2,'exp'=2] {'core'}, dimensions={0} | all-to-all | bytes 4718592 | tf_op jit(solution)/shard_map/all_to_all | solution.py:440
  320.2 13.2 %all-to-all-done.12 = bf16[4,128,1152]{2,1,0:T(8,128)(2,1)S(1)} async-done(((bf16[4,128,1152]{2,1,0:T(8,128)(2,1)}), bf16[4,128,1152]{2,1,0:T(8,128)(2,1)S(1)}, u32[]{:S(2)}, u32[]{:S(2)}) %all-to-all-start.12) | async-done | bytes 1179680 | tf_op jit(solution)/shard_map/all_to_all | solution.py:440
  342.7 24.8 %collective-permute-done.12 = bf16[512,1536]{1,0:T(8,128)(2,1)} collective-permute-done((bf16[512,1536]{1,0:T(8,128)(2,1)}, bf16[512,1536]{1,0:T(8,128)(2,1)}, u32[]{:S(2)}, u32[]{:S(2)}) %collective-permute-start.12) | collective-permute-done | bytes 1572896 | tf_op jit(solution)/shard_map/ppermute | solution.py:468
  367.5 31.9 %collective-permute-done.13 = bf16[512,1536]{1,0:T(8,128)(2,1)} collective-permute-done((bf16[512,1536]{1,0:T(8,128)(2,1)}, bf16[512,1536]{1,0:T(8,128)(2,1)}, u32[]{:S(2)}, u32[]{:S(2)}) %collective-permute-start.13) | collective-permute-done | bytes 1572896 | tf_op jit(solution)/shard_map/ppermute | solution.py:468
  407.6 11.3 %shard_map.398 = (bf16[1024,384]{1,0:T(8,128)(2,1)}, bf16[8,128,1024]{2,1,0:T(8,128)(2,1)S(1)}) custom-call(bf16[1024,1152]{1,0:T(8,128)(2,1)S(1)} %copy-done.1, bf16[1024,512]{1,0:T(8,128)(2,1)S(1)} %bitcast.164, f32[1024,256]{1,0:T(8,128)S(1)} %copy-done.3, f32[8,128,128]{2,1,0:T(8,128)S(1)} %copy-done.10, bf16[1024,256]{1,0:T(8,128)(2,1)S(1)} %copy-done.34, ...), custom_call_target="tpu_custom_call" | custom-call | flops 1610612736 | bytes 6291456 | tf_op jit(solution)/shard_map/pallas_call | solution.py:1085
  418.9 5.4 %all_to_all.90 = bf16[2,512,1024]{2,1,0:T(8,128)(2,1)S(1)} all-to-all(bf16[2,512,1024]{2,1,0:T(8,128)(2,1)S(1)} %bitcast.174), channel_id=1, replica_groups=mesh['a'=4,'r'=2,'core'=2,'exp'=2] {'core'}, dimensions={0} | all-to-all | bytes 4194304 | tf_op jit(solution)/shard_map/all_to_all | solution.py:440
  430.1 11.8 %collective-permute-done.20 = bf16[64,1536]{1,0:T(8,128)(2,1)S(1)} collective-permute-done((bf16[64,1536]{1,0:T(8,128)(2,1)S(1)}, bf16[64,1536]{1,0:T(8,128)(2,1)S(1)}, u32[]{:S(2)}, u32[]{:S(2)}) %collective-permute-start.20) | collective-permute-done | bytes 196640 | tf_op jit(solution)/shard_map/ppermute | solution.py:468
  455.9 6.3 %all-to-all-done.15 = bf16[4,128,1024]{2,1,0:T(8,128)(2,1)S(1)} async-done(((bf16[4,128,1024]{2,1,0:T(8,128)(2,1)}), bf16[4,128,1024]{2,1,0:T(8,128)(2,1)S(1)}, u32[]{:S(2)}, u32[]{:S(2)}) %all-to-all-start.15) | async-done | bytes 1048608 | tf_op jit(solution)/shard_map/all_to_all | solution.py:440
  463.2 6.1 %all-to-all-start.16 = ((bf16[32,32,384]{2,1,0:T(8,128)(2,1)}), bf16[32,32,384]{2,1,0:T(8,128)(2,1)S(1)}, u32[]{:S(2)}, u32[]{:S(2)}) async-start(bf16[32,32,384]{2,1,0:T(8,128)(2,1)} %bitcast.79), calls=%async_computation.16 | async-start | bytes 1572864 | tf_op jit(solution)/shard_map/all_to_all | solution.py:440
  469.3 7.7 %multiply_subtract_fusion = (f32[8,64,1024]{2,1,0:T(8,128)}, f32[8,64,1024]{2,1,0:T(8,128)}, f32[8,64,1024]{2,1,0:T(8,128)}) fusion(f32[8,64,1024]{2,1,0:T(8,128)} %param.41, f32[8,64,1536]{2,1,0:T(8,128)} %convert_element_type.264, f32[8,64,1024]{2,1,0:T(8,128)} %param.42, f32[8,64,1024]{2,1,0:T(8,128)} %param.43), kind=kLoop, calls=%fused_computation.33 | loop fusion | flops 7864320 | bytes 14680064 | tf_op jit(solution)/shard_map/sub | solution.py:62
  478.4 11.2 %all-to-all-done.16.refs_0_ = bf16[32,32,384]{2,1,0:T(8,128)(2,1)S(1)} async-done(((bf16[32,32,384]{2,1,0:T(8,128)(2,1)}), bf16[32,32,384]{2,1,0:T(8,128)(2,1)S(1)}, u32[]{:S(2)}, u32[]{:S(2)}) %all-to-all-start.16) | async-done | bytes 786464 | tf_op jit(solution)/shard_map/all_to_all | solution.py:440
  (310 shorter events, 163.9 us)
Async XLA Ops:
  11.1 16.3 %all-to-all-start = ((bf16[8,32,384]{2,1,0:T(8,128)(2,1)}), bf16[8,32,384]{2,1,0:T(8,128)(2,1)S(1)}, u32[]{:S(2)}, u32[]{:S(2)}) async-start(bf16[8,32,384]{2,1,0:T(8,128)(2,1)} %copy.91), calls=%async_computation | async-start | bytes 393216 | tf_op jit(solution)/shard_map/all_to_all | solution.py:440
  16.2 68.0 %all-gather.3.cloned.1.call-start = ((), (), s32[]{:S(2)}) async-start(), calls=%async_computation.17 | async-start | bytes 2654208 | tf_op jit(solution)/shard_map/all_gather | solution.py:1139
  29.0 17.5 %collective-permute-start.1 = (bf16[64,1536]{1,0:T(8,128)(2,1)}, bf16[64,1536]{1,0:T(8,128)(2,1)}, u32[]{:S(2)}, u32[]{:S(2)}) collective-permute-start(bf16[64,1536]{1,0:T(8,128)(2,1)} %get-tuple-element.89), channel_id=1, source_target_pairs={{0,16},{2,18},{8,24},{10,26},{16,0},{18,2},{24,8},{26,10},{1,17},{... | collective-permute-start | bytes 589832 | tf_op jit(solution)/shard_map/ppermute | solution.py:468
  31.6 16.5 %collective-permute-start.2 = (bf16[64,1536]{1,0:T(8,128)(2,1)}, bf16[64,1536]{1,0:T(8,128)(2,1)}, u32[]{:S(2)}, u32[]{:S(2)}) collective-permute-start(bf16[64,1536]{1,0:T(8,128)(2,1)} %get-tuple-element.90), channel_id=1, source_target_pairs={{0,24},{2,26},{8,16},{10,18},{16,8},{18,10},{24,0},{26,2},{1,25},{... | collective-permute-start | bytes 589832 | tf_op jit(solution)/shard_map/ppermute | solution.py:468
  31.8 17.2 %collective-permute-start.3 = (bf16[64,1536]{1,0:T(8,128)(2,1)}, bf16[64,1536]{1,0:T(8,128)(2,1)}, u32[]{:S(2)}, u32[]{:S(2)}) collective-permute-start(bf16[64,1536]{1,0:T(8,128)(2,1)} %get-tuple-element.91), channel_id=1, source_target_pairs={{0,2},{2,0},{8,10},{10,8},{16,18},{18,16},{24,26},{26,24},{1,3},{3... | collective-permute-start | bytes 589832 | tf_op jit(solution)/shard_map/ppermute | solution.py:468
  31.8 18.2 %collective-permute-start.4 = (bf16[64,1536]{1,0:T(8,128)(2,1)}, bf16[64,1536]{1,0:T(8,128)(2,1)}, u32[]{:S(2)}, u32[]{:S(2)}) collective-permute-start(bf16[64,1536]{1,0:T(8,128)(2,1)} %get-tuple-element.92), channel_id=1, source_target_pairs={{0,10},{2,8},{8,2},{10,0},{16,26},{18,24},{24,18},{26,16},{1,11},{... | collective-permute-start | bytes 589832 | tf_op jit(solution)/shard_map/ppermute | solution.py:468
  33.7 61.4 %all-to-all-start.1 = ((bf16[4,256,512]{2,1,0:T(8,128)(2,1)}), bf16[4,256,512]{2,1,0:T(8,128)(2,1)S(1)}, u32[]{:S(2)}, u32[]{:S(2)}) async-start(bf16[4,256,512]{2,1,0:T(8,128)(2,1)} %broadcast_in_dim.133), calls=%async_computation.1 | async-start | bytes 2097152 | tf_op jit(solution)/shard_map/all_to_all | solution.py:440
  38.6 157.3 %all-gather.5.cloned.1.call-start = ((), (), s32[]{:S(2)}) async-start(), calls=%async_computation.18 | async-start | bytes 7864320 | tf_op jit(solution)/shard_map/all_gather | solution.py:1193
  39.2 44.9 %collective-permute-start.5 = (bf16[64,1536]{1,0:T(8,128)(2,1)S(1)}, bf16[64,1536]{1,0:T(8,128)(2,1)S(1)}, u32[]{:S(2)}, u32[]{:S(2)}) collective-permute-start(bf16[64,1536]{1,0:T(8,128)(2,1)S(1)} %copy-done.69), channel_id=1, source_target_pairs={{0,18},{2,16},{8,26},{10,24},{16,2},{18,0},{24,10},{26,8},{1,19},{... | collective-permute-start | bytes 589832 | tf_op jit(solution)/shard_map/ppermute | solution.py:468
  46.5 37.7 %collective-permute-start.6 = (bf16[64,1536]{1,0:T(8,128)(2,1)S(1)}, bf16[64,1536]{1,0:T(8,128)(2,1)S(1)}, u32[]{:S(2)}, u32[]{:S(2)}) collective-permute-start(bf16[64,1536]{1,0:T(8,128)(2,1)S(1)} %copy-done.70), channel_id=1, source_target_pairs={{0,26},{2,24},{8,18},{10,16},{16,10},{18,8},{24,2},{26,0},{1,27},{... | collective-permute-start | bytes 589832 | tf_op jit(solution)/shard_map/ppermute | solution.py:468
  99.9 27.2 %all-to-all-start.2 = ((bf16[4,128,1024]{2,1,0:T(8,128)(2,1)}), bf16[4,128,1024]{2,1,0:T(8,128)(2,1)}, u32[]{:S(2)}, u32[]{:S(2)}) async-start(bf16[4,128,1024]{2,1,0:T(8,128)(2,1)} %broadcast_in_dim.143), calls=%async_computation.2 | async-start | bytes 2097152 | tf_op jit(solution)/shard_map/all_to_all | solution.py:440
  104.1 54.1 %collective-permute-start.7 = (bf16[128,1024]{0,1:T(8,128)(2,1)}, bf16[128,1024]{0,1:T(8,128)(2,1)}, u32[]{:S(2)}, u32[]{:S(2)}) collective-permute-start(bf16[128,1024]{0,1:T(8,128)(2,1)} %fusion.18), channel_id=1, source_target_pairs={{0,8},{8,0},{16,24},{24,16},{1,9},{9,1},{17,25},{25,17},{2,10},{10... | collective-permute-start | bytes 786440 | tf_op jit(solution)/shard_map/ppermute | solution.py:468
  109.0 51.0 %collective-permute-start.8 = (bf16[128,1024]{0,1:T(8,128)(2,1)}, bf16[128,1024]{0,1:T(8,128)(2,1)}, u32[]{:S(2)}, u32[]{:S(2)}) collective-permute-start(bf16[128,1024]{0,1:T(8,128)(2,1)} %fusion.18), channel_id=1, source_target_pairs={{0,16},{8,24},{16,0},{24,8},{1,17},{9,25},{17,1},{25,9},{2,18},{10... | collective-permute-start | bytes 786440 | tf_op jit(solution)/shard_map/ppermute | solution.py:468
  110.1 53.8 %collective-permute-start.9 = (bf16[128,1024]{0,1:T(8,128)(2,1)}, bf16[128,1024]{0,1:T(8,128)(2,1)}, u32[]{:S(2)}, u32[]{:S(2)}) collective-permute-start(bf16[128,1024]{0,1:T(8,128)(2,1)} %fusion.18), channel_id=1, source_target_pairs={{0,24},{8,16},{16,8},{24,0},{1,25},{9,17},{17,9},{25,1},{2,26},{10... | collective-permute-start | bytes 786440 | tf_op jit(solution)/shard_map/ppermute | solution.py:468
  150.7 37.1 %all-to-all-start.5 = ((bf16[4,128,1152]{2,1,0:T(8,128)(2,1)}), bf16[4,128,1152]{2,1,0:T(8,128)(2,1)}, u32[]{:S(2)}, u32[]{:S(2)}) async-start(bf16[4,128,1152]{2,1,0:T(8,128)(2,1)} %copy-done.27), calls=%async_computation.5 | async-start | bytes 2359296 | tf_op jit(solution)/shard_map/all_to_all | solution.py:440
  231.2 33.5 %all-to-all-start.8 = ((bf16[4,128,1152]{2,1,0:T(8,128)(2,1)}), bf16[4,128,1152]{2,1,0:T(8,128)(2,1)}, u32[]{:S(2)}, u32[]{:S(2)}) async-start(bf16[4,128,1152]{2,1,0:T(8,128)(2,1)} %bitcast.185), calls=%async_computation.8 | async-start | bytes 2359296 | tf_op jit(solution)/shard_map/all_to_all | solution.py:440
  237.8 20.8 %collective-permute-start.11 = (bf16[512,1024]{1,0:T(8,128)(2,1)}, bf16[512,1024]{1,0:T(8,128)(2,1)}, u32[]{:S(2)}, u32[]{:S(2)}) collective-permute-start(bf16[512,1024]{1,0:T(8,128)(2,1)} %dynamic-slice_bitcast_fusion), channel_id=1, source_target_pairs={{0,2},{2,0},{1,3},{3,1},{4,6},{6,4},{5,7},{7,5},{8,10},{10,8},{9,1... | collective-permute-start | bytes 3145736 | tf_op jit(solution)/shard_map/ppermute | solution.py:468
  264.7 29.8 %all-to-all-start.9 = ((bf16[4,128,1024]{2,1,0:T(8,128)(2,1)}), bf16[4,128,1024]{2,1,0:T(8,128)(2,1)}, u32[]{:S(2)}, u32[]{:S(2)}) async-start(bf16[4,128,1024]{2,1,0:T(8,128)(2,1)} %bitcast.189), calls=%async_computation.9 | async-start | bytes 2097152 | tf_op jit(solution)/shard_map/all_to_all | solution.py:440
  312.7 20.7 %all-to-all-start.12 = ((bf16[4,128,1152]{2,1,0:T(8,128)(2,1)}), bf16[4,128,1152]{2,1,0:T(8,128)(2,1)S(1)}, u32[]{:S(2)}, u32[]{:S(2)}) async-start(bf16[4,128,1152]{2,1,0:T(8,128)(2,1)} %bitcast.58), calls=%async_computation.12 | async-start | bytes 2359296 | tf_op jit(solution)/shard_map/all_to_all | solution.py:440
  316.4 51.1 %collective-permute-start.12 = (bf16[512,1536]{1,0:T(8,128)(2,1)}, bf16[512,1536]{1,0:T(8,128)(2,1)}, u32[]{:S(2)}, u32[]{:S(2)}) collective-permute-start(bf16[512,1536]{1,0:T(8,128)(2,1)} %get-tuple-element.127), channel_id=1, source_target_pairs={{0,5},{1,4},{4,1},{5,0},{2,7},{3,6},{6,3},{7,2},{8,13},{9,12},{12,... | collective-permute-start | bytes 4718600 | tf_op jit(solution)/shard_map/ppermute | solution.py:468
  319.3 80.2 %collective-permute-start.13 = (bf16[512,1536]{1,0:T(8,128)(2,1)}, bf16[512,1536]{1,0:T(8,128)(2,1)}, u32[]{:S(2)}, u32[]{:S(2)}) collective-permute-start(bf16[512,1536]{1,0:T(8,128)(2,1)} %get-tuple-element.128), channel_id=1, source_target_pairs={{0,1},{1,0},{4,5},{5,4},{2,3},{3,2},{6,7},{7,6},{8,9},{9,8},{12,13... | collective-permute-start | bytes 4718600 | tf_op jit(solution)/shard_map/ppermute | solution.py:468
  319.8 79.7 %collective-permute-start.14 = (bf16[512,1536]{1,0:T(8,128)(2,1)}, bf16[512,1536]{1,0:T(8,128)(2,1)}, u32[]{:S(2)}, u32[]{:S(2)}) collective-permute-start(bf16[512,1536]{1,0:T(8,128)(2,1)} %get-tuple-element.129), channel_id=1, source_target_pairs={{0,4},{1,5},{4,0},{5,1},{2,6},{3,7},{6,2},{7,3},{8,12},{9,13},{12,... | collective-permute-start | bytes 4718600 | tf_op jit(solution)/shard_map/ppermute | solution.py:468
  334.2 65.3 %all-to-all-start.13 = ((bf16[4,32,1152]{2,1,0:T(8,128)(2,1)}), bf16[4,32,1152]{2,1,0:T(8,128)(2,1)S(1)}, u32[]{:S(2)}, u32[]{:S(2)}) async-start(bf16[4,32,1152]{2,1,0:T(8,128)(2,1)} %bitcast.59), calls=%async_computation.13 | async-start | bytes 589824 | tf_op jit(solution)/shard_map/all_to_all | solution.py:440
  403.1 22.6 %collective-permute-start.15 = (bf16[64,1536]{1,0:T(8,128)(2,1)S(1)}, bf16[64,1536]{1,0:T(8,128)(2,1)S(1)}, u32[]{:S(2)}, u32[]{:S(2)}) collective-permute-start(bf16[64,1536]{1,0:T(8,128)(2,1)S(1)} %get-tuple-element.170), channel_id=1, source_target_pairs={{0,8},{2,10},{8,0},{10,2},{16,24},{18,26},{24,16},{26,18},{1,9},{3... | collective-permute-start | bytes 589832 | tf_op jit(solution)/shard_map/ppermute | solution.py:468
  403.2 24.4 %collective-permute-start.16 = (bf16[64,1536]{1,0:T(8,128)(2,1)S(1)}, bf16[64,1536]{1,0:T(8,128)(2,1)S(1)}, u32[]{:S(2)}, u32[]{:S(2)}) collective-permute-start(bf16[64,1536]{1,0:T(8,128)(2,1)S(1)} %get-tuple-element.169), channel_id=1, source_target_pairs={{0,16},{2,18},{8,24},{10,26},{16,0},{18,2},{24,8},{26,10},{1,17},{... | collective-permute-start | bytes 589832 | tf_op jit(solution)/shard_map/ppermute | solution.py:468
  405.2 24.8 %collective-permute-start.17 = (bf16[64,1536]{1,0:T(8,128)(2,1)S(1)}, bf16[64,1536]{1,0:T(8,128)(2,1)S(1)}, u32[]{:S(2)}, u32[]{:S(2)}) collective-permute-start(bf16[64,1536]{1,0:T(8,128)(2,1)S(1)} %get-tuple-element.168), channel_id=1, source_target_pairs={{0,24},{2,26},{8,16},{10,18},{16,8},{18,10},{24,0},{26,2},{1,25},{... | collective-permute-start | bytes 589832 | tf_op jit(solution)/shard_map/ppermute | solution.py:468
  407.6 22.5 %collective-permute-start.18 = (bf16[64,1536]{1,0:T(8,128)(2,1)S(1)}, bf16[64,1536]{1,0:T(8,128)(2,1)S(1)}, u32[]{:S(2)}, u32[]{:S(2)}) collective-permute-start(bf16[64,1536]{1,0:T(8,128)(2,1)S(1)} %get-tuple-element.167), channel_id=1, source_target_pairs={{0,2},{2,0},{8,10},{10,8},{16,18},{18,16},{24,26},{26,24},{1,3},{3... | collective-permute-start | bytes 589832 | tf_op jit(solution)/shard_map/ppermute | solution.py:468
  407.6 22.5 %collective-permute-start.19 = (bf16[64,1536]{1,0:T(8,128)(2,1)S(1)}, bf16[64,1536]{1,0:T(8,128)(2,1)S(1)}, u32[]{:S(2)}, u32[]{:S(2)}) collective-permute-start(bf16[64,1536]{1,0:T(8,128)(2,1)S(1)} %get-tuple-element.166), channel_id=1, source_target_pairs={{0,10},{2,8},{8,2},{10,0},{16,26},{18,24},{24,18},{26,16},{1,11},{... | collective-permute-start | bytes 589832 | tf_op jit(solution)/shard_map/ppermute | solution.py:468
  425.7 16.2 %collective-permute-start.20 = (bf16[64,1536]{1,0:T(8,128)(2,1)S(1)}, bf16[64,1536]{1,0:T(8,128)(2,1)S(1)}, u32[]{:S(2)}, u32[]{:S(2)}) collective-permute-start(bf16[64,1536]{1,0:T(8,128)(2,1)S(1)} %get-tuple-element.165), channel_id=1, source_target_pairs={{0,18},{2,16},{8,26},{10,24},{16,2},{18,0},{24,10},{26,8},{1,19},{... | collective-permute-start | bytes 589832 | tf_op jit(solution)/shard_map/ppermute | solution.py:468
  427.6 14.4 %collective-permute-start.21 = (bf16[64,1536]{1,0:T(8,128)(2,1)S(1)}, bf16[64,1536]{1,0:T(8,128)(2,1)S(1)}, u32[]{:S(2)}, u32[]{:S(2)}) collective-permute-start(bf16[64,1536]{1,0:T(8,128)(2,1)S(1)} %get-tuple-element.164), channel_id=1, source_target_pairs={{0,26},{2,24},{8,18},{10,16},{16,10},{18,8},{24,2},{26,0},{1,27},{... | collective-permute-start | bytes 589832 | tf_op jit(solution)/shard_map/ppermute | solution.py:468
  444.0 18.2 %all-to-all-start.15 = ((bf16[4,128,1024]{2,1,0:T(8,128)(2,1)}), bf16[4,128,1024]{2,1,0:T(8,128)(2,1)S(1)}, u32[]{:S(2)}, u32[]{:S(2)}) async-start(bf16[4,128,1024]{2,1,0:T(8,128)(2,1)} %bitcast.186), calls=%async_computation.15 | async-start | bytes 2097152 | tf_op jit(solution)/shard_map/all_to_all | solution.py:440
  463.2 26.4 %all-to-all-start.16 = ((bf16[32,32,384]{2,1,0:T(8,128)(2,1)}), bf16[32,32,384]{2,1,0:T(8,128)(2,1)S(1)}, u32[]{:S(2)}, u32[]{:S(2)}) async-start(bf16[32,32,384]{2,1,0:T(8,128)(2,1)} %bitcast.79), calls=%async_computation.16 | async-start | bytes 1572864 | tf_op jit(solution)/shard_map/all_to_all | solution.py:440
  (81 other events, 547.7 us)
Sparse Core Ops, SparseCore 0:
  19.5 30.7 all-gather.2
  95.2 84.3 all-gather.4
